TPU v7x, 32 devices: a whole 2x2x4 slice. The times are simulated.
32 devices in a mesh: rows: 8 (over z, x), tm: 4 (over y, core).
Axes of the slice: x: 2, y: 2, z: 4, core: 2. Of those that a mesh axis runs over, the one named last changes fastest.
Arguments:
- frames: bfloat16 [16, 16, 32, 256], P('tm', 'rows'), may hold values from -45 to 45, as said below
- norm_gain: float32 [256], replicated, may hold values from 0.1 to 1.9
- conv_weight: bfloat16 [3, 3, 3, 256, 256], replicated, may hold values from -0.078125 to 0.078125
- conv_bias: float32 [256], replicated, may hold values from -3 to 3
- latent_grad: bfloat16 [16, 8, 16, 256], P('tm', None, 'rows'), may hold values from -6 to 6
Outputs:
- latent: bfloat16 [16, 8, 16, 256], P('tm', None, 'rows')
- frames_grad: bfloat16 [16, 16, 32, 256], P('tm', 'rows')
- weight_grad: float32 [3, 3, 3, 256, 256], P(None, None, None, 'tm')
- gain_grad: float32 [256], P('tm')
- bias_grad: float32 [256], P('tm')
Inputs may be any that keep to these rules, and one draw needn't show every extreme that they name: `frames`: features of the clip.
All inputs are finite; a program needn't handle non-finite values.
Results may differ from a plain program's by a relative error of at most 0.0045.
Values may be sent and summed in bfloat16 or wider, within the bound.
No kernel may reach another device: no remote copies, remote signals or barrier semaphores. Data moves between devices by JAX's collectives and lax.ppermute only.
A program may use at most 128 MiB of HBM per device.

v0:
```python
import functools

import jax
import jax.numpy as jnp
from jax import lax
from jax.experimental import pallas as pl
from jax.experimental.pallas import tpu as pltpu
from jax.sharding import PartitionSpec as P

EPS = 1e-06
TAPS = [(a, b, c) for a in range(3) for b in range(3) for c in range(3)]
VMEM_LIMIT = 20 * 1024 * 1024
VMEM_LIMIT_WIDE = 60 * 1024 * 1024
WORK = 1200


def shifted(value, axis, steps):
    count = lax.axis_size(axis)
    leading, last = (max(0, -steps), min(count, count - steps))
    return lax.ppermute(value, axis, [(source, source + steps) for source in range(leading, last)])


def contract_out(grad_piece, weight_tap):
    return lax.dot_general(
        grad_piece, weight_tap, (((1,), (1,)), ((), ())), preferred_element_type=jnp.float32
    )


def reduced_form(frames, norm_gain, conv_weight, conv_bias, latent_grad):
    signal = frames.astype(jnp.float32)
    inv_rms = lax.rsqrt(jnp.mean(signal * signal, axis=-1, keepdims=True) + EPS)
    unit = signal * inv_rms
    normed = unit * norm_gain
    hidden = jax.nn.silu(normed).astype(jnp.bfloat16)
    frame_count, row_count, col_count, channels = hidden.shape
    lat_rows = row_count // 2
    lat_cols = col_count // 2
    cached = shifted(hidden[frame_count - 2 :], "tm", 1)
    stacked = jnp.concatenate([cached, hidden], axis=0)
    row_under = shifted(stacked[:, :1], "rows", -1)
    extended = jnp.concatenate([stacked, row_under], axis=1)
    extended = jnp.pad(extended, ((0, 0), (0, 0), (0, 1), (0, 0)))
    grad_rows = lax.all_to_all(latent_grad, "rows", split_axis=1, concat_axis=2, tiled=True)
    grad_flat = grad_rows.reshape(-1, channels)
    running = jnp.zeros((frame_count * lat_rows * lat_cols, channels), jnp.float32)
    blocks = []
    for tap_t, tap_r, tap_c in TAPS:
        window_piece = extended[
            tap_t : tap_t + frame_count,
            tap_r : tap_r + 2 * lat_rows : 2,
            tap_c : tap_c + 2 * lat_cols : 2,
        ]
        window_piece = window_piece.reshape(-1, channels)
        running = running + jnp.dot(
            window_piece, conv_weight[tap_t, tap_r, tap_c], preferred_element_type=jnp.float32
        )
        blocks.append(
            lax.dot_general(
                window_piece,
                grad_flat,
                (((0,), (0,)), ((), ())),
                preferred_element_type=jnp.float32,
            )
        )
    latent_rows = (
        (running + conv_bias)
        .reshape(frame_count, lat_rows, lat_cols, channels)
        .astype(jnp.bfloat16)
    )
    latent = lax.all_to_all(latent_rows, "rows", split_axis=2, concat_axis=1, tiled=True)
    weight_local = jnp.stack(blocks).reshape(3, 3, 3, channels, channels)
    bias_local = jnp.sum(grad_flat.astype(jnp.float32), axis=0)
    following = shifted(grad_rows[:2], "tm", -1)
    grad_ext = jnp.concatenate([grad_rows, following], axis=0)
    above_row = shifted(grad_ext, "rows", 1)
    grad_ext = jnp.concatenate([above_row, grad_ext], axis=1)
    grad_ext = jnp.pad(grad_ext, ((0, 0), (0, 0), (1, 0), (0, 0)))
    parity_sums = {}
    for tap_t, tap_r, tap_c in TAPS:
        row_start = 1 - tap_r // 2
        col_start = 1 - tap_c // 2
        grad_piece = grad_ext[
            2 - tap_t : 2 - tap_t + frame_count,
            row_start : row_start + lat_rows,
            col_start : col_start + lat_cols,
        ]
        term = contract_out(grad_piece.reshape(-1, channels), conv_weight[tap_t, tap_r, tap_c])
        label = (tap_r % 2, tap_c % 2)
        parity_sums[label] = parity_sums[label] + term if label in parity_sums else term
    shaped = {}
    for label in parity_sums:
        shaped[label] = parity_sums[label].reshape(frame_count, lat_rows, lat_cols, channels)
    even_rows = jnp.stack([shaped[0, 0], shaped[0, 1]], axis=3)
    odd_rows = jnp.stack([shaped[1, 0], shaped[1, 1]], axis=3)
    hidden_grad = jnp.stack([even_rows, odd_rows], axis=2).reshape(
        frame_count, row_count, col_count, channels
    )
    sigma = jax.nn.sigmoid(normed)
    normed_grad = hidden_grad * sigma * (1.0 + normed * (1.0 - sigma))
    gain_local = jnp.sum(normed_grad * unit, axis=(0, 1, 2))
    unit_grad = normed_grad * norm_gain
    frames_grad = inv_rms * (unit_grad - unit * jnp.mean(unit_grad * unit, axis=-1, keepdims=True))
    totals = lax.psum((weight_local, gain_local, bias_local), "rows")
    weight_grad, gain_grad, bias_grad = (
        lax.psum_scatter(totals[0], "tm", scatter_dimension=3, tiled=True),
        lax.psum_scatter(totals[1], "tm", scatter_dimension=0, tiled=True),
        lax.psum_scatter(totals[2], "tm", scatter_dimension=0, tiled=True),
    )
    return (latent, frames_grad.astype(jnp.bfloat16), weight_grad, gain_grad, bias_grad)


def partners(value, axis, bits):
    count = lax.axis_size(axis)
    return lax.ppermute(value, axis, [(source, source ^ bits) for source in range(count)])


def exchanged(value, axis, gate=None):
    count = lax.axis_size(axis)
    blocks = {0: value}
    for k in range(1, count):
        if k & (k - 1) == 0:
            blocks[k] = partners(value, axis, k)
    if gate is not None:
        held = [k for k in blocks if k > 1]
        blocks.update(zip(held, gate([blocks[k] for k in held])))
    for k in range(1, count):
        low = k & -k
        if k != low:
            blocks[k] = partners(blocks[k - low], axis, low)
    return [blocks[k] for k in range(count)]


def mm(left, right):
    return jnp.dot(left, right, preferred_element_type=jnp.float32)


def mm_t(left, right):
    return lax.dot_general(
        left, right, (((1,), (1,)), ((), ())), preferred_element_type=jnp.float32
    )


def normalised(frames, gain):
    signal = frames.astype(jnp.float32)
    inv_rms = lax.rsqrt(jnp.mean(signal * signal, axis=-1, keepdims=True) + EPS)
    unit = signal * inv_rms
    return inv_rms, unit, unit * gain


def hidden_kernel(F, J, T, place, frames, vectors, planes, frames_copy, vectors_copy, *rest):
    sends, tmp = rest[:T], rest[T]
    frames_copy[...] = frames[...]
    vectors_copy[...] = vectors[...]
    channels = frames.shape[1]
    part = channels // T
    _, _, normed = normalised(frames[...], vectors[0:1])
    value = normed / (1.0 + jnp.exp(-normed))
    tmp[0] = value[:, : channels // 2]
    tmp[1] = value[:, channels // 2 :]
    block = place[1]
    for rp in range(2):
        pair = []
        for cp in range(2):
            rows = [
                jnp.concatenate(
                    [
                        tmp[half, pl.ds((t * 2 + rp) * 2 * J + cp, J, stride=2), :]
                        for half in range(2)
                    ],
                    axis=1,
                )
                for t in range(F)
            ]
            plane = jnp.concatenate(rows, axis=0)
            pair.append(plane)
            plane = plane.astype(jnp.bfloat16)
            planes[rp, cp] = plane
            late = plane[(F - 2) * J :]
            for k in range(1, T, 2):
                for half in range(2):
                    at = (((rp * 2 + cp) * 2) + half) * 2 * J
                    lanes = slice(half * channels // 2, (half + 1) * channels // 2)
                    sends[k][2 * F * J + at : 2 * F * J + at + 2 * J] = late[:, lanes]
        pieces = [
            jnp.concatenate([p[:, d * part : (d + 1) * part] for p in pair], axis=1)
            for d in range(T)
        ]
        for k in range(T):
            chosen = pieces[0]
            for d in range(1, T):
                chosen = jnp.where(block == d ^ k, pieces[d], chosen)
            sends[k][rp * F * J : (rp + 1) * F * J] = chosen.astype(jnp.bfloat16)


def head_kernel(rows, _, grad_rows, head, passed):
    passed[...] = grad_rows[...]
    for s in range(grad_rows.shape[0]):
        head[s] = grad_rows[s, :rows, :]


def join_kernel(F, J, T, place, planes, *refs):
    messages, (joined, cached, under, blocks) = refs[:T], refs[T:]
    span = F * J
    block = place[1]
    for k in range(T):
        at = pl.multiple_of((block ^ k) * span, 16)
        for rp in range(2):
            blocks[rp, pl.ds(at, span), :] = messages[k][rp * span : (rp + 1) * span, :]
    for rp in range(2):
        joined[rp] = blocks[rp].T
    for rp in range(2):
        for cp in range(2):
            halves = []
            for half in range(2):
                start = 2 * span + ((rp * 2 + cp) * 2 + half) * 2 * J
                value = jnp.zeros((2 * J, messages[1].shape[1]), jnp.bfloat16)
                for k in range(1, T, 2):
                    found = (block > 0) & (block ^ k == block - 1)
                    value = jnp.where(found, messages[k][start : start + 2 * J, :], value)
                halves.append(value)
            before = jnp.concatenate(halves, axis=1)
            cached[rp, cp] = before
            if rp == 0:
                under[cp, : 2 * J] = before
                under[cp, 2 * J :] = planes[0, cp]


def permutation(shape, meet):
    row = lax.broadcasted_iota(jnp.int32, shape, 0)
    col = lax.broadcasted_iota(jnp.int32, shape, 1)
    return jnp.where(meet(row, col), 1.0, 0.0).astype(jnp.bfloat16)


def slice_of(value, block, k, T):
    part = value.shape[1] // T
    chosen = value[:, :part]
    for d in range(1, T):
        chosen = jnp.where(block == d ^ k, value[:, d * part : (d + 1) * part], chosen)
    return chosen


def shard_order(J, R, rows, first, moved):
    jl = J // R
    return permutation(
        (rows * 2 * J, R * 2 * J),
        lambda o, s: (o // (2 * J) + first == s // jl % R)
        & (o // J % 2 == s // (jl * R) % 2)
        & (o % J == s // (2 * jl * R) * jl + s % jl + moved),
    )


def shard_rows(source, start, count):
    return jnp.concatenate(
        [source[s, start : start + count, :] for s in range(source.shape[0])], axis=0
    )


def gate_kernel(*refs):
    pass


def slab_kernel(
    F, J, R, T, slot, place, planes, cached, under, weight_hbm, frames, vectors, gathered, following,
    out, frames_grad, weight, near, ext, tmp, sem,
):
    row, block = place[0], place[1]
    channels = frames.shape[1]
    span = F * J
    gain, bias = vectors[0:1], vectors[1:2]
    fetches = [
        pltpu.make_async_copy(weight_hbm.at[pl.ds(a * 9, 9)], weight.at[pl.ds(a * 9, 9)], sem.at[a])
        for a in range(3)
    ]
    for copy in fetches:
        copy.start()

    orders = [shard_order(J, R, 2, row - 1, moved) for moved in range(2)]
    for pair in range(F // 2 + 1):
        if pair < F // 2:
            source = shard_rows(gathered, pair * 2 * J, 2 * J)
        else:
            source = shard_rows(following, 0, 2 * J)
        for moved in range(2):
            value = mm(orders[moved], source).astype(jnp.bfloat16)
            for i in range(2):
                near[moved, i, pair * 2 * J : (pair + 1) * 2 * J, :] = value[
                    i * 2 * J : (i + 1) * 2 * J
                ]

    rows = (F + 2) * J
    last = lax.broadcasted_iota(jnp.int32, (rows, 1), 0) % J == J - 1
    for b in range(3):
        for cp in range(2):
            if b == 2:
                full = under[cp]
            else:
                full = jnp.concatenate([cached[b, cp], planes[b, cp]], axis=0)
            ext[b, cp] = full
            if cp == 0:
                moved = pltpu.roll(full.astype(jnp.float32), rows - 1, 0)
                ext[b, 2] = jnp.where(last, 0.0, moved).astype(jnp.bfloat16)

    latent = jnp.zeros((span, channels), jnp.float32)
    sums = {}
    for n, (a, b, c) in enumerate(TAPS):
        if n % 9 == 0:
            fetches[a].wait()
        latent = latent + mm(ext[b, c, a * J : (a + F) * J, :], weight[n])
        piece = near[c // 2, 1 - b // 2, (2 - a) * J : (2 - a + F) * J, :]
        term = mm_t(piece, weight[n])
        key = (b % 2, c % 2)
        sums[key] = sums[key] + term if key in sums else term
    for (rp, cp), value in sums.items():
        for t in range(F):
            for half in range(2):
                lanes = slice(half * channels // 2, (half + 1) * channels // 2)
                tmp[half, pl.ds((t * 2 + rp) * 2 * J + cp, J, stride=2), :] = value[
                    t * J : (t + 1) * J, lanes
                ]
    hidden_grad = jnp.concatenate([tmp[0], tmp[1]], axis=1)
    inv_rms, unit, normed = normalised(frames[...], gain)
    sigma = 1.0 / (1.0 + jnp.exp(-normed))
    normed_grad = hidden_grad * sigma * (1.0 + normed * (1.0 - sigma))
    gain_part = jnp.sum(normed_grad * unit, axis=0, keepdims=True)
    unit_grad = normed_grad * gain
    mean = jnp.mean(unit_grad * unit, axis=-1, keepdims=True)
    frames_grad[...] = (inv_rms * (unit_grad - unit * mean)).astype(jnp.bfloat16)

    jl = J // R
    used = span // R
    blocks = out.shape[0] // (R * slot)
    order = permutation(
        (R * blocks * slot, span),
        lambda o, s: (o % slot < used)
        & (o // slot % blocks == block)
        & (o % slot // jl == s // J)
        & (o // (slot * blocks) * jl + o % jl == s % J),
    )
    value = mm(order, (latent + bias).astype(jnp.bfloat16))
    line = lax.broadcasted_iota(jnp.int32, (R * blocks * slot, 1), 0) % slot
    rest = gain_part
    for n in range(3):
        term = rest.astype(jnp.bfloat16).astype(jnp.float32)
        rest = rest - term
        value = jnp.where(line == used + n, term, value)
    out[...] = value.astype(jnp.bfloat16)


def finish_kernel(F, R, T, used, place, received, *refs):
    latent, gain = refs[-2:]
    block = place[1]
    slot = received.shape[2]
    jl = used // F
    value = jnp.zeros(received.shape[2:], jnp.float32)
    for r in range(R):
        for t in range(T):
            value = value + received[r, t].astype(jnp.float32)
    line = lax.broadcasted_iota(jnp.int32, (slot, 1), 0)
    value = jnp.where((line >= used) & (line < used + 3), value, 0.0)
    gain[...] = slice_of(jnp.sum(value, axis=0, keepdims=True), block, 0, T)
    source = jnp.concatenate([received[r, block] for r in range(R)], axis=0)
    order = permutation(
        (R * used, R * slot),
        lambda o, s: (s % slot < used)
        & (o // (R * jl) == s % slot // jl)
        & (o // jl % R == s // slot)
        & (o % jl == s % jl),
    )
    latent[...] = mm(order, source).astype(jnp.bfloat16)


def order_kernel(F, J, R, T, place, _, *refs):
    gathered, (grads, bias_sum) = refs[:T], refs[T:]
    channels = grads.shape[-1]
    span = F * J
    depth = T * span
    block = place[1]
    grads[:, :, depth:, :] = jnp.zeros((2, R, 2 * J, channels), jnp.bfloat16)
    orders = [shard_order(J, R, R, 0, moved) for moved in range(2)]
    total = jnp.zeros((1, channels), jnp.float32)
    for k in range(T):
        for pair in range(F // 2):
            source = shard_rows(gathered[k], pair * 2 * J, 2 * J)
            total = total + jnp.sum(source.astype(jnp.float32), axis=0, keepdims=True)
            at = pl.multiple_of((block ^ k) * span + pair * 2 * J, 16)
            for moved in range(2):
                value = mm(orders[moved], source).astype(jnp.bfloat16)
                for i in range(R):
                    grads[moved, i, pl.ds(at, 2 * J), :] = value[i * 2 * J : (i + 1) * 2 * J]
    bias_sum[...] = slice_of(total, block, 0, T)


def weight_kernel(F, J, R, T, part, place, grads, *refs):
    hidden = refs[:R]
    out_hbm, out, even, odd, sem = refs[R:]
    channels = grads.shape[-1]
    depth = T * F * J
    lanes = 2 * part
    row = place[0]
    even[:, R * depth :] = jnp.zeros((lanes, depth), jnp.bfloat16)
    for k in range(R):
        at = pl.multiple_of((row ^ k) * depth, 128)
        for rp, turned in ((0, even), (1, odd)):
            turned[:, pl.ds(at, depth)] = hidden[k][rp]
    leaving = []
    for a in range(3):
        start = (2 - a) * J
        for moved in range(2):
            right = grads[moved, :, start : start + depth, :].reshape(R * depth, channels)
            size = part if moved else lanes
            left = jnp.concatenate(
                [even[:size, : R * depth], odd[:size, :], even[:size, depth:]], axis=0
            )
            value = mm(left, right)
            for b in range(3):
                if moved:
                    out[(a * 3 + b) * 3 + 2] = value[b * part : (b + 1) * part]
                else:
                    for cp in range(2):
                        at = b * lanes + cp * part
                        out[(a * 3 + b) * 3 + cp] = value[at : at + part]
        taps = pl.ds(a * 9, 9)
        leaving.append(pltpu.make_async_copy(out.at[taps], out_hbm.at[taps], sem.at[a]))
        leaving[a].start()
    for copy in leaving:
        copy.wait()


def call(kernel, outs, scratch, flops, moved, places, aliases={}, limit=VMEM_LIMIT):
    kinds = {"s": pltpu.SMEM, "v": pltpu.VMEM, "h": pltpu.HBM, "a": pl.ANY}
    specs = [pl.BlockSpec(memory_space=kinds[p]) for p in places]
    count = len(places) - len(outs)
    return pl.pallas_call(
        kernel,
        out_shape=[jax.ShapeDtypeStruct(s, d) for s, d in outs],
        in_specs=specs[:count],
        out_specs=specs[count:],
        scratch_shapes=scratch,
        input_output_aliases=aliases,
        compiler_params=pltpu.CompilerParams(vmem_limit_bytes=limit),
        cost_estimate=pl.CostEstimate(flops=flops, bytes_accessed=moved, transcendentals=0),
    )


def gathered_form(frames, norm_gain, conv_weight, conv_bias, latent_grad):
    bf16, f32 = jnp.bfloat16, jnp.float32
    F, row_count, col_count, C = frames.shape
    R, T = lax.axis_size("rows"), lax.axis_size("tm")
    J = col_count // 2
    span = F * J
    part = C // T
    used = span // R
    slot = -(-(used + 3) // 16) * 16
    vectors = jnp.stack([norm_gain, conv_bias])
    flat = frames.reshape(-1, C)
    weight = conv_weight.reshape(27, C, C)
    place = jnp.stack([lax.axis_index("rows"), lax.axis_index("tm")]).astype(jnp.int32)

    own = latent_grad.reshape(1, -1, C)
    grad_rows = lax.all_to_all(
        jnp.broadcast_to(own, (R,) + own.shape[1:]), "rows", 0, 0, tiled=True
    )

    sizes = [(2 * span + (16 * J if k % 2 else 0), 2 * part) for k in range(T)]
    planes, frames_copy, vectors, *sends = call(
        functools.partial(hidden_kernel, F, J, T),
        [((2, 2, span, C), bf16), (flat.shape, bf16), ((2, C), f32)]
        + [(size, bf16) for size in sizes],
        [pltpu.VMEM((2, 4 * span, C // 2), f32)],
        60 * WORK * span * C, 16 * span * C, "svv" + "v" * (T + 3),
    )(place, flat, vectors)
    head, grad_rows = call(
        functools.partial(head_kernel, 2 * J),
        [((R, 2 * J, C), bf16), (grad_rows.shape, bf16)],
        [], R * span * C, R * span * C, "avvv",
    )(frames_copy, grad_rows)
    messages = [sends[0]] + [partners(sends[k], "tm", k) for k in range(1, T)]
    joined, cached, under = call(
        functools.partial(join_kernel, F, J, T),
        [
            ((2, 2 * part, T * span), bf16),
            ((2, 2, 2 * J, C), bf16),
            ((2, 2 * J + span, C), bf16),
        ],
        [pltpu.VMEM((2, T * span, 2 * part), bf16)],
        30 * WORK * span * C, 16 * span * C, "sv" + "v" * T + "vvv",
    )(place, planes, *messages)
    under = shifted(under, "rows", -1)
    following = shifted(head, "tm", -1)
    packed, frames_grad = call(
        functools.partial(slab_kernel, F, J, R, T, slot),
        [((R * T * slot, C), bf16), ((4 * span, C), bf16)],
        [
            pltpu.VMEM((27, C, C), bf16),
            pltpu.VMEM((2, 2, (F + 2) * J, C), bf16),
            pltpu.VMEM((3, 3, (F + 2) * J, C), bf16),
            pltpu.VMEM((2, 4 * span, C // 2), f32),
            pltpu.SemaphoreType.DMA((3,)),
        ],
        2 * 54 * span * C * C, 2 * 27 * C * C, "svvvhvvvv" + "vv",
        limit=VMEM_LIMIT_WIDE,
    )(place, planes, cached, under, weight, frames_copy, vectors, grad_rows, following)

    later = {}

    def after_slab(blocks):
        through = [packed] + blocks
        shapes = [(b.shape, bf16) for b in through]
        count = len(through)
        aliases = {n: n for n in range(count)}
        later["packed"], *blocks = call(
            gate_kernel, shapes, [], 0, 0, "a" * (2 * count), aliases
        )(*through)
        return blocks

    hidden_all = exchanged(joined, "rows", after_slab)
    grad_all = exchanged(grad_rows, "tm")

    packed = lax.all_to_all(later["packed"].reshape(R * T, slot, C), ("rows", "tm"), 0, 0, tiled=True)
    latent, gain_grad = call(
        functools.partial(finish_kernel, F, R, T, used),
        [((span, C), bf16), ((1, part), f32)],
        [], R * slot * C, R * slot * C, "sv" + "a" * (R // 2) + "vv",
    )(place, packed.reshape(R, T, slot, C), *hidden_all[1::2])

    grads, bias_sum = call(
        functools.partial(order_kernel, F, J, R, T),
        [((2, R, (F * T + 2) * J, C), bf16), ((1, part), f32)],
        [],
        90 * WORK * span * C, 2 * R * T * span * C, "sa" + "v" * (T + 2),
    )(place, gain_grad, *grad_all)
    (weight_grad,) = call(
        functools.partial(weight_kernel, F, J, R, T, part),
        [((27, part, C), f32)],
        [
            pltpu.VMEM((27, part, C), f32),
            pltpu.VMEM((2 * part, (R + 1) * T * span), bf16),
            pltpu.VMEM((2 * part, R * T * span), bf16),
            pltpu.SemaphoreType.DMA((3,)),
        ],
        200 * WORK * span * C, 8 * 27 * part * C, "sv" + "v" * R + "h",
    )(place, grads, *hidden_all)

    return (
        latent.reshape(F, R, J // R, C),
        frames_grad.reshape(frames.shape),
        weight_grad.reshape(3, 3, 3, part, C),
        gain_grad.reshape(part),
        bias_sum.reshape(part),
    )


def on_device(frames, norm_gain, conv_weight, conv_bias, latent_grad):
    rows, shares = lax.axis_size("rows"), lax.axis_size("tm")
    operand_bytes = 2 * rows * shares * (frames.size // shares + latent_grad.size)
    result_bytes = 4 * conv_weight.size
    powers = (rows & (rows - 1)) == 0 and (shares & (shares - 1)) == 0
    if powers and frames.shape[1] == 2 and operand_bytes <= result_bytes:
        form = gathered_form
    else:
        form = reduced_form
    return form(frames, norm_gain, conv_weight, conv_bias, latent_grad)


def solution(mesh):
    placed = (P("tm", "rows", None, None), P(), P(), P(), P("tm", None, "rows", None))
    return jax.shard_map(
        on_device,
        mesh=mesh,
        in_specs=placed,
        out_specs=(
            P("tm", None, "rows", None),
            P("tm", "rows", None, None),
            P(None, None, None, "tm", None),
            P("tm"),
            P("tm"),
        ),
        check_vma=False,
    )
```

profile of v0, /device:TPU:0, one launch (start us, length us, event | category | flops | bytes accessed | tf_op | source)
XLA Modules:
  0.0 66.7 jit_solution(2571954348814355378)
XLA Ops:
  0.6 0.8 %broadcast_in_dim.7 = bf16[64,256]{1,0:T(8,128)(2,1)S(1)} reshape(bf16[4,8,2,256]{3,2,1,0:T(2,128)(2,1)} %param.9) | data formatting | bytes 65536 | tf_op jit(solution)/shard_map/broadcast_in_dim | solution.py:461
  1.4 0.7 %broadcast_in_dim.8 = bf16[8,64,256]{2,1,0:T(8,128)(2,1)} broadcast(bf16[64,256]{1,0:T(8,128)(2,1)S(1)} %broadcast_in_dim.7), dimensions={1,2} | broadcast | bytes 294912 | tf_op jit(solution)/shard_map/broadcast_in_dim | solution.py:461
  2.1 7.3 %all-to-all-start = ((bf16[8,64,256]{2,1,0:T(8,128)(2,1)}), bf16[8,64,256]{2,1,0:T(8,128)(2,1)S(1)}, u32[]{:S(2)}, u32[]{:S(2)}) async-start(bf16[8,64,256]{2,1,0:T(8,128)(2,1)} %broadcast_in_dim.8), calls=%async_computation | async-start | bytes 524288 | tf_op jit(solution)/shard_map/all_to_all | solution.py:460
  9.4 0.1 pad_add_fusion.place
  9.5 0.7 %pad_maximum_fusion.vectors = f32[2,256]{1,0:T(2,128)S(1)} fusion(f32[1,256]{1,0:T(1,128)} %bitcast.17, f32[1,256]{1,0:T(1,128)} %bitcast.18), kind=kLoop, calls=%fused_computation | loop fusion | flops 512 | bytes 4096 | tf_op jit(solution)/shard_map/stack | solution.py:454
  10.2 0.9 %copy-done.10 = bf16[4,2,32,256]{3,2,1,0:T(8,128)(2,1)S(1)} copy-done((bf16[4,2,32,256]{3,2,1,0:T(8,128)(2,1)S(1)}, bf16[4,2,32,256]{3,2,1,0:T(8,128)(2,1)}, u32[]{:S(2)}) %copy-start.10) | copy-done | bytes 131096
  11.1 0.8 %shard_map.92 = (bf16[2,2,64,256]{3,2,1,0:T(8,128)(2,1)S(1)}, bf16[256,256]{1,0:T(8,128)(2,1)S(1)}, f32[2,256]{1,0:T(2,128)S(1)}, bf16[128,128]{1,0:T(8,128)(2,1...) custom-call(s32[2]{0:T(128)S(1)} %pad_add_fusion.place, ...), custom_call_target="tpu_custom_call" | custom-call | flops 1179648000 | bytes 262144 | tf_op jit(solution)/shard_map/pallas_call | solution.py:465
  11.9 0.0 copy-start.7
  11.9 0.6 copy-done.7
  12.5 0.0 collective-permute-start
  12.5 1.6 %collective-permute-start.2 = (bf16[384,128]{1,0:T(8,128)(2,1)S(1)}, bf16[384,128]{1,0:T(8,128)(2,1)S(1)}, u32[]{:S(2)}, u32[]{:S(2)}) collective-permute-start(bf16[384,128]{1,0:T(8,128)(2,1)S(1)} %get-tuple-element.30), channel_id=1, source_target_pairs={{0,3},{1,2},{2,1},{3,0},{4,7},{5,6},{6,5},{7,4},{8,11},{9,10},{10,... | collective-permute-start | bytes 294920 | tf_op jit(solution)/shard_map/ppermute | solution.py:114
  14.1 0.5 collective-permute-start.1
  14.7 3.6 %all-to-all-done.grad_rows = bf16[8,64,256]{2,1,0:T(8,128)(2,1)S(1)} async-done(((bf16[8,64,256]{2,1,0:T(8,128)(2,1)}), bf16[8,64,256]{2,1,0:T(8,128)(2,1)S(1)}, u32[]{:S(2)}, u32[]{:S(2)}) %all-to-all-start) | async-done | bytes 262176 | tf_op jit(solution)/shard_map/all_to_all | solution.py:460
  18.3 0.0 copy-start.3
  18.3 1.3 %collective-permute-start.4 = (bf16[8,32,256]{2,1,0:T(8,128)(2,1)S(1)}, bf16[8,32,256]{2,1,0:T(8,128)(2,1)S(1)}, u32[]{:S(2)}, u32[]{:S(2)}) collective-permute-start(bf16[8,32,256]{2,1,0:T(8,128)(2,1)S(1)} %get-tuple-element.36), channel_id=1, source_target_pairs={{1,0},{2,1},{3,2},{5,4},{6,5},{7,6},{9,8},{10,9},{11,10},{13,12},{... | collective-permute-start | bytes 393224 | tf_op jit(solution)/shard_map/ppermute | solution.py:20
  19.6 0.0 collective-permute-done.1.refs_2_
  19.7 0.0 collective-permute-done.refs_1_
  19.7 0.0 collective-permute-done.2.refs_3_
  19.7 0.0 copy-done.8
  19.7 0.6 shard_map.93
  20.3 0.0 copy-start.6
  20.3 0.6 copy-done.6
  21.0 1.3 %collective-permute-start.3 = (bf16[2,96,256]{2,1,0:T(8,128)(2,1)S(1)}, bf16[2,96,256]{2,1,0:T(8,128)(2,1)S(1)}, u32[]{:S(2)}, u32[]{:S(2)}) collective-permute-start(bf16[2,96,256]{2,1,0:T(8,128)(2,1)S(1)} %get-tuple-element.32), channel_id=1, source_target_pairs={{4,0},{8,4},{12,8},{16,12},{20,16},{24,20},{28,24},{5,1},{9,5},{13... | collective-permute-start | bytes 294920 | tf_op jit(solution)/shard_map/ppermute | solution.py:20
  22.2 3.7 %collective-permute-start.6 = (bf16[2,128,256]{2,1,0:T(8,128)(2,1)S(1)}, bf16[2,128,256]{2,1,0:T(8,128)(2,1)S(1)}, u32[]{:S(2)}, u32[]{:S(2)}) collective-permute-start(bf16[2,128,256]{2,1,0:T(8,128)(2,1)S(1)} %get-tuple-element.38.refs_0_), channel_id=1, source_target_pairs={{0,16},{4,20},{8,24},{12,28},{16,0},{20,4},{24,8},{28,12},{1,17},{... | collective-permute-start | bytes 393224 | tf_op jit(solution)/shard_map/ppermute | solution.py:114
  25.9 1.5 %collective-permute-start.5 = (bf16[2,128,256]{2,1,0:T(8,128)(2,1)S(1)}, bf16[2,128,256]{2,1,0:T(8,128)(2,1)S(1)}, u32[]{:S(2)}, u32[]{:S(2)}) collective-permute-start(bf16[2,128,256]{2,1,0:T(8,128)(2,1)S(1)} %get-tuple-element.38.refs_0_), channel_id=1, source_target_pairs={{0,8},{4,12},{8,0},{12,4},{16,24},{20,28},{24,16},{28,20},{1,9},{5... | collective-permute-start | bytes 393224 | tf_op jit(solution)/shard_map/ppermute | solution.py:114
  27.4 1.5 %collective-permute-start.13 = (bf16[8,64,256]{2,1,0:T(8,128)(2,1)S(1)}, bf16[8,64,256]{2,1,0:T(8,128)(2,1)S(1)}, u32[]{:S(2)}, u32[]{:S(2)}) collective-permute-start(bf16[8,64,256]{2,1,0:T(8,128)(2,1)S(1)} %get-tuple-element.35.gathered.refs_0_), channel_id=1, source_target_pairs={{0,2},{1,3},{2,0},{3,1},{4,6},{5,7},{6,4},{7,5},{8,10},{9,11},{10,... | collective-permute-start | bytes 786440 | tf_op jit(solution)/shard_map/ppermute | solution.py:114
  28.9 0.0 collective-permute-done.3.under
  28.9 0.0 collective-permute-done.4.following
  28.9 0.0 copy-start.12
  29.0 0.0 copy-done.2
  29.0 0.0 copy-done.5
  29.0 0.0 copy-done.3
  29.0 0.6 copy-done.13
  29.6 0.1 copy-done.12
  29.6 5.3 %shard_map.95 = (bf16[512,256]{1,0:T(8,128)(2,1)}, bf16[256,256]{1,0:T(8,128)(2,1)}) custom-call(s32[2]{0:T(128)} %copy-done.8, bf16[2,2,64,256]{3,2,1,0:T(8,128)(2,1)} %copy-done.5, bf16[2,2,32,256]{3,2,1,0:T(8,128)(2,1)} %copy-done.6, bf16[2,96,256]{2,1,0:T(8,128)(2,1)} %copy-done.13, bf16[27,256,256]{2,1,0:T(8,128)(2,1)} %bitcast.16, ...), custom_call_target="tpu_custom_call" | custom-call | flops 452984832 | bytes 3538944 | tf_op jit(solution)/shard_map/pallas_call | solution.py:490
  34.9 0.0 collective-permute-done.6.refs_2_
  34.9 0.0 collective-permute-done.5.refs_1_
  34.9 0.0 copy-start
  34.9 0.9 %copy-done = bf16[512,256]{1,0:T(8,128)(2,1)S(1)} copy-done((bf16[512,256]{1,0:T(8,128)(2,1)S(1)}, bf16[512,256]{1,0:T(8,128)(2,1)}, u32[]{:S(2)}) %copy-start) | copy-done | bytes 262168
  35.9 0.7 %copy-done.1 = bf16[512,256]{1,0:T(8,128)(2,1)} copy-done((bf16[512,256]{1,0:T(8,128)(2,1)}, bf16[512,256]{1,0:T(8,128)(2,1)S(1)}, u32[]{:S(2)}) %copy-start.1) | copy-done | bytes 262168
  36.6 4.4 %all-to-all-start.1 = ((bf16[32,16,256]{2,1,0:T(8,128)(2,1)}), bf16[32,16,256]{2,1,0:T(8,128)(2,1)S(1)}, u32[]{:S(2)}, u32[]{:S(2)}) async-start(bf16[32,16,256]{2,1,0:T(8,128)(2,1)} %bitcast.12), calls=%async_computation.1 | async-start | bytes 524288 | tf_op jit(solution)/shard_map/all_to_all | solution.py:519
  41.0 1.8 %collective-permute-start.7 = (bf16[2,128,256]{2,1,0:T(8,128)(2,1)S(1)}, bf16[2,128,256]{2,1,0:T(8,128)(2,1)S(1)}, u32[]{:S(2)}, u32[]{:S(2)}) collective-permute-start(bf16[2,128,256]{2,1,0:T(8,128)(2,1)S(1)} %get-tuple-element.38.refs_0_), channel_id=1, source_target_pairs={{0,4},{4,0},{8,12},{12,8},{16,20},{20,16},{24,28},{28,24},{1,5},{5... | collective-permute-start | bytes 393224 | tf_op jit(solution)/shard_map/ppermute | solution.py:114
  42.8 1.5 %collective-permute-start.10 = (bf16[2,128,256]{2,1,0:T(8,128)(2,1)S(1)}, bf16[2,128,256]{2,1,0:T(8,128)(2,1)S(1)}, u32[]{:S(2)}, u32[]{:S(2)}) collective-permute-start(bf16[2,128,256]{2,1,0:T(8,128)(2,1)S(1)} %get-tuple-element.41.refs_4_), channel_id=1, source_target_pairs={{0,8},{4,12},{8,0},{12,4},{16,24},{20,28},{24,16},{28,20},{1,9},{5... | collective-permute-start | bytes 393224 | tf_op jit(solution)/shard_map/ppermute | solution.py:114
  44.3 0.0 collective-permute-start.12
  44.3 0.0 collective-permute-done.13.refs_2_
  44.3 0.5 collective-permute-start.14
  44.8 0.6 collective-permute-start.9
  45.4 4.2 %collective-permute-done.7.refs_0_.refs_1_ = bf16[2,128,256]{2,1,0:T(8,128)(2,1)S(1)} collective-permute-done((bf16[2,128,256]{2,1,0:T(8,128)(2,1)S(1)}, bf16[2,128,256]{2,1,0:T(8,128)(2,1)S(1)}, u32[]{:S(2)}, u32[]{:S(2)}) %collective-permute-start.7) | collective-permute-done | bytes 131104 | tf_op jit(solution)/shard_map/ppermute | solution.py:114
  49.6 0.9 %collective-permute-start.8 = (bf16[2,128,256]{2,1,0:T(8,128)(2,1)S(1)}, bf16[2,128,256]{2,1,0:T(8,128)(2,1)S(1)}, u32[]{:S(2)}, u32[]{:S(2)}) collective-permute-start(bf16[2,128,256]{2,1,0:T(8,128)(2,1)S(1)} %get-tuple-element.40.refs_2_), channel_id=1, source_target_pairs={{0,4},{4,0},{8,12},{12,8},{16,20},{20,16},{24,28},{28,24},{1,5},{5... | collective-permute-start | bytes 393224 | tf_op jit(solution)/shard_map/ppermute | solution.py:114
  50.5 0.4 collective-permute-done.10.refs_6_
  50.9 1.5 %collective-permute-start.11 = (bf16[2,128,256]{2,1,0:T(8,128)(2,1)S(1)}, bf16[2,128,256]{2,1,0:T(8,128)(2,1)S(1)}, u32[]{:S(2)}, u32[]{:S(2)}) collective-permute-start(bf16[2,128,256]{2,1,0:T(8,128)(2,1)S(1)} %collective-permute-done.10.refs_6_), channel_id=1, source_target_pairs={{0,4},{4,0},{8,12},{12,8},{16,20},{20,16},{24,28},{28,24},{1,5},{5... | collective-permute-start | bytes 393224 | tf_op jit(solution)/shard_map/ppermute | solution.py:114
  52.4 3.7 %collective-permute-done.8.refs_1_.refs_3_ = bf16[2,128,256]{2,1,0:T(8,128)(2,1)S(1)} collective-permute-done((bf16[2,128,256]{2,1,0:T(8,128)(2,1)S(1)}, bf16[2,128,256]{2,1,0:T(8,128)(2,1)S(1)}, u32[]{:S(2)}, u32[]{:S(2)}) %collective-permute-start.8) | collective-permute-done | bytes 131104 | tf_op jit(solution)/shard_map/ppermute | solution.py:114
  56.0 0.0 collective-permute-done.9.refs_2_.refs_5_
  56.0 1.9 %collective-permute-done.11.refs_3_.refs_7_ = bf16[2,128,256]{2,1,0:T(8,128)(2,1)S(1)} collective-permute-done((bf16[2,128,256]{2,1,0:T(8,128)(2,1)S(1)}, bf16[2,128,256]{2,1,0:T(8,128)(2,1)S(1)}, u32[]{:S(2)}, u32[]{:S(2)}) %collective-permute-start.11) | collective-permute-done | bytes 131104 | tf_op jit(solution)/shard_map/ppermute | solution.py:114
  57.9 0.0 all-to-all-done.1
  57.9 0.0 copy-done.9
  57.9 1.4 %shard_map.97 = (bf16[64,256]{1,0:T(8,128)(2,1)S(1)}, f32[1,64]{1,0:T(1,128)}) custom-call(s32[2]{0:T(128)S(1)} %copy-done.9, bf16[8,4,16,256]{3,2,1,0:T(8,128)(2,1)S(1)} %bitcast.13, bf16[2,128,256]{2,1,0:T(8,128)(2,1)S(1)} %collective-permute-done.7.refs_0_.refs_1_, bf16[2,128,256]{2,1,0:T(8,128)(2,1)S(1)} %collective-permute-done.8.refs_1_.refs_3_, ...), custom_call_target="tpu_custom_call" | custom-call | flops 32768 | bytes 32768 | tf_op jit(solution)/shard_map/pallas_call | solution.py:520
  59.3 0.6 reshape.43
  59.9 0.0 collective-permute-done.12.refs_1_
  59.9 0.0 collective-permute-done.14.refs_3_
  59.9 0.9 %copy-done.4 = bf16[8,64,256]{2,1,0:T(8,128)(2,1)S(1)} copy-done((bf16[8,64,256]{2,1,0:T(8,128)(2,1)S(1)}, bf16[8,64,256]{2,1,0:T(8,128)(2,1)}, u32[]{:S(2)}) %copy-start.4) | copy-done | bytes 262168
  60.9 0.7 copy-done.11
  61.5 1.8 %shard_map.98 = (bf16[2,8,288,256]{3,2,1,0:T(8,128)(2,1)S(1)}, f32[1,64]{1,0:T(1,128)}) custom-call(s32[2]{0:T(128)S(1)} %copy-done.9, f32[1,64]{1,0:T(1,128)S(1)} %copy-done.11, bf16[8,64,256]{2,1,0:T(8,128)(2,1)S(1)} %copy-done.4, bf16[8,64,256]{2,1,0:T(8,128)(2,1)S(1)} %collective-permute-done.12.refs_1_, ...), custom_call_target="tpu_custom_call" | custom-call | flops 1769472000 | bytes 1048576 | tf_op jit(solution)/shard_map/pallas_call | solution.py:526
  63.3 3.4 %shard_map.99 = f32[27,64,256]{2,1,0:T(8,128)} custom-call(s32[2]{0:T(128)S(1)} %copy-done.9, bf16[2,8,288,256]{3,2,1,0:T(8,128)(2,1)S(1)} %get-tuple-element.45.grads, bf16[2,128,256]{2,1,0:T(8,128)(2,1)S(1)} %get-tuple-element.38.refs_0_, bf16[2,128,256]{2,1,0:T(8,128)(2,1)S(1)} %collective-permute-done.7.refs_0_.refs_1_, ...), custom_call_target="tpu_custom_call" | custom-call | flops 3932160000 | bytes 3538944 | tf_op jit(solution)/shard_map/pallas_call | solution.py:532
  (11 shorter events, 0.0 us)
Async XLA Ops:
  2.1 16.2 %all-to-all-start = ((bf16[8,64,256]{2,1,0:T(8,128)(2,1)}), bf16[8,64,256]{2,1,0:T(8,128)(2,1)S(1)}, u32[]{:S(2)}, u32[]{:S(2)}) async-start(bf16[8,64,256]{2,1,0:T(8,128)(2,1)} %broadcast_in_dim.8), calls=%async_computation | async-start | bytes 524288 | tf_op jit(solution)/shard_map/all_to_all | solution.py:460
  9.5 10.2 %copy-start.8 = (s32[2]{0:T(128)}, s32[2]{0:T(128)S(1)}, u32[]{:S(2)}) copy-start(s32[2]{0:T(128)S(1)} %pad_add_fusion.place) | copy-start | bytes 28
  10.2 0.9 %copy-start.10 = (bf16[4,2,32,256]{3,2,1,0:T(8,128)(2,1)S(1)}, bf16[4,2,32,256]{3,2,1,0:T(8,128)(2,1)}, u32[]{:S(2)}) copy-start(bf16[4,2,32,256]{3,2,1,0:T(8,128)(2,1)} %param.5) | copy-start | bytes 393220
  11.9 0.6 copy-start.7
  12.5 16.4 %copy-start.2 = (bf16[256,256]{1,0:T(8,128)(2,1)}, bf16[256,256]{1,0:T(8,128)(2,1)S(1)}, u32[]{:S(2)}) copy-start(bf16[256,256]{1,0:T(8,128)(2,1)S(1)} %get-tuple-element.33._.frames) | copy-start | bytes 393220
  12.5 16.5 %copy-start.5 = (bf16[2,2,64,256]{3,2,1,0:T(8,128)(2,1)}, bf16[2,2,64,256]{3,2,1,0:T(8,128)(2,1)S(1)}, u32[]{:S(2)}) copy-start(bf16[2,2,64,256]{3,2,1,0:T(8,128)(2,1)S(1)} %get-tuple-element.26.planes) | copy-start | bytes 393220
  12.5 7.1 %collective-permute-start = (bf16[384,128]{1,0:T(8,128)(2,1)S(1)}, bf16[384,128]{1,0:T(8,128)(2,1)S(1)}, u32[]{:S(2)}, u32[]{:S(2)}) collective-permute-start(bf16[384,128]{1,0:T(8,128)(2,1)S(1)} %get-tuple-element.28), channel_id=1, source_target_pairs={{0,1},{1,0},{2,3},{3,2},{4,5},{5,4},{6,7},{7,6},{8,9},{9,8},{10,11... | collective-permute-start | bytes 294920 | tf_op jit(solution)/shard_map/ppermute | solution.py:114
  12.5 7.2 %collective-permute-start.2 = (bf16[384,128]{1,0:T(8,128)(2,1)S(1)}, bf16[384,128]{1,0:T(8,128)(2,1)S(1)}, u32[]{:S(2)}, u32[]{:S(2)}) collective-permute-start(bf16[384,128]{1,0:T(8,128)(2,1)S(1)} %get-tuple-element.30), channel_id=1, source_target_pairs={{0,3},{1,2},{2,1},{3,0},{4,7},{5,6},{6,5},{7,4},{8,11},{9,10},{10,... | collective-permute-start | bytes 294920 | tf_op jit(solution)/shard_map/ppermute | solution.py:114
  14.1 5.5 %collective-permute-start.1 = (bf16[128,128]{1,0:T(8,128)(2,1)S(1)}, bf16[128,128]{1,0:T(8,128)(2,1)S(1)}, u32[]{:S(2)}, u32[]{:S(2)}) collective-permute-start(bf16[128,128]{1,0:T(8,128)(2,1)S(1)} %get-tuple-element.29), channel_id=1, source_target_pairs={{0,2},{1,3},{2,0},{3,1},{4,6},{5,7},{6,4},{7,5},{8,10},{9,11},{10,... | collective-permute-start | bytes 98312 | tf_op jit(solution)/shard_map/ppermute | solution.py:114
  18.3 10.6 %copy-start.3 = (bf16[8,64,256]{2,1,0:T(8,128)(2,1)}, bf16[8,64,256]{2,1,0:T(8,128)(2,1)S(1)}, u32[]{:S(2)}) copy-start(bf16[8,64,256]{2,1,0:T(8,128)(2,1)S(1)} %get-tuple-element.35.gathered.refs_0_) | copy-start | bytes 786436
  18.3 10.6 %collective-permute-start.4 = (bf16[8,32,256]{2,1,0:T(8,128)(2,1)S(1)}, bf16[8,32,256]{2,1,0:T(8,128)(2,1)S(1)}, u32[]{:S(2)}, u32[]{:S(2)}) collective-permute-start(bf16[8,32,256]{2,1,0:T(8,128)(2,1)S(1)} %get-tuple-element.36), channel_id=1, source_target_pairs={{1,0},{2,1},{3,2},{5,4},{6,5},{7,6},{9,8},{10,9},{11,10},{13,12},{... | collective-permute-start | bytes 393224 | tf_op jit(solution)/shard_map/ppermute | solution.py:20
  20.3 0.6 copy-start.6
  21.0 8.0 %collective-permute-start.3 = (bf16[2,96,256]{2,1,0:T(8,128)(2,1)S(1)}, bf16[2,96,256]{2,1,0:T(8,128)(2,1)S(1)}, u32[]{:S(2)}, u32[]{:S(2)}) collective-permute-start(bf16[2,96,256]{2,1,0:T(8,128)(2,1)S(1)} %get-tuple-element.32), channel_id=1, source_target_pairs={{4,0},{8,4},{12,8},{16,12},{20,16},{24,20},{28,24},{5,1},{9,5},{13... | collective-permute-start | bytes 294920 | tf_op jit(solution)/shard_map/ppermute | solution.py:20
  22.2 12.7 %collective-permute-start.6 = (bf16[2,128,256]{2,1,0:T(8,128)(2,1)S(1)}, bf16[2,128,256]{2,1,0:T(8,128)(2,1)S(1)}, u32[]{:S(2)}, u32[]{:S(2)}) collective-permute-start(bf16[2,128,256]{2,1,0:T(8,128)(2,1)S(1)} %get-tuple-element.38.refs_0_), channel_id=1, source_target_pairs={{0,16},{4,20},{8,24},{12,28},{16,0},{20,4},{24,8},{28,12},{1,17},{... | collective-permute-start | bytes 393224 | tf_op jit(solution)/shard_map/ppermute | solution.py:114
  25.9 9.0 %collective-permute-start.5 = (bf16[2,128,256]{2,1,0:T(8,128)(2,1)S(1)}, bf16[2,128,256]{2,1,0:T(8,128)(2,1)S(1)}, u32[]{:S(2)}, u32[]{:S(2)}) collective-permute-start(bf16[2,128,256]{2,1,0:T(8,128)(2,1)S(1)} %get-tuple-element.38.refs_0_), channel_id=1, source_target_pairs={{0,8},{4,12},{8,0},{12,4},{16,24},{20,28},{24,16},{28,20},{1,9},{5... | collective-permute-start | bytes 393224 | tf_op jit(solution)/shard_map/ppermute | solution.py:114
  27.4 16.9 %collective-permute-start.13 = (bf16[8,64,256]{2,1,0:T(8,128)(2,1)S(1)}, bf16[8,64,256]{2,1,0:T(8,128)(2,1)S(1)}, u32[]{:S(2)}, u32[]{:S(2)}) collective-permute-start(bf16[8,64,256]{2,1,0:T(8,128)(2,1)S(1)} %get-tuple-element.35.gathered.refs_0_), channel_id=1, source_target_pairs={{0,2},{1,3},{2,0},{3,1},{4,6},{5,7},{6,4},{7,5},{8,10},{9,11},{10,... | collective-permute-start | bytes 786440 | tf_op jit(solution)/shard_map/ppermute | solution.py:114
  28.9 0.6 copy-start.13
  28.9 0.7 %copy-start.12 = (bf16[8,32,256]{2,1,0:T(8,128)(2,1)}, bf16[8,32,256]{2,1,0:T(8,128)(2,1)S(1)}, u32[]{:S(2)}) copy-start(bf16[8,32,256]{2,1,0:T(8,128)(2,1)S(1)} %collective-permute-done.4.following) | copy-start | bytes 393220
  29.6 28.3 %copy-start.9 = (s32[2]{0:T(128)S(1)}, s32[2]{0:T(128)}, u32[]{:S(2)}) copy-start(s32[2]{0:T(128)} %copy-done.8) | copy-start | bytes 28
  34.9 1.0 %copy-start = (bf16[512,256]{1,0:T(8,128)(2,1)S(1)}, bf16[512,256]{1,0:T(8,128)(2,1)}, u32[]{:S(2)}) copy-start(bf16[512,256]{1,0:T(8,128)(2,1)} %get-tuple-element.37.refs_0_) | copy-start | bytes 786436
  35.9 0.7 %copy-start.1 = (bf16[512,256]{1,0:T(8,128)(2,1)}, bf16[512,256]{1,0:T(8,128)(2,1)S(1)}, u32[]{:S(2)}) copy-start(bf16[512,256]{1,0:T(8,128)(2,1)S(1)} %get-tuple-element.39) | copy-start | bytes 786436
  36.6 21.3 %all-to-all-start.1 = ((bf16[32,16,256]{2,1,0:T(8,128)(2,1)}), bf16[32,16,256]{2,1,0:T(8,128)(2,1)S(1)}, u32[]{:S(2)}, u32[]{:S(2)}) async-start(bf16[32,16,256]{2,1,0:T(8,128)(2,1)} %bitcast.12), calls=%async_computation.1 | async-start | bytes 524288 | tf_op jit(solution)/shard_map/all_to_all | solution.py:519
  41.0 8.6 %collective-permute-start.7 = (bf16[2,128,256]{2,1,0:T(8,128)(2,1)S(1)}, bf16[2,128,256]{2,1,0:T(8,128)(2,1)S(1)}, u32[]{:S(2)}, u32[]{:S(2)}) collective-permute-start(bf16[2,128,256]{2,1,0:T(8,128)(2,1)S(1)} %get-tuple-element.38.refs_0_), channel_id=1, source_target_pairs={{0,4},{4,0},{8,12},{12,8},{16,20},{20,16},{24,28},{28,24},{1,5},{5... | collective-permute-start | bytes 393224 | tf_op jit(solution)/shard_map/ppermute | solution.py:114
  42.8 8.1 %collective-permute-start.10 = (bf16[2,128,256]{2,1,0:T(8,128)(2,1)S(1)}, bf16[2,128,256]{2,1,0:T(8,128)(2,1)S(1)}, u32[]{:S(2)}, u32[]{:S(2)}) collective-permute-start(bf16[2,128,256]{2,1,0:T(8,128)(2,1)S(1)} %get-tuple-element.41.refs_4_), channel_id=1, source_target_pairs={{0,8},{4,12},{8,0},{12,4},{16,24},{20,28},{24,16},{28,20},{1,9},{5... | collective-permute-start | bytes 393224 | tf_op jit(solution)/shard_map/ppermute | solution.py:114
  44.3 15.6 %collective-permute-start.12 = (bf16[8,64,256]{2,1,0:T(8,128)(2,1)}, bf16[8,64,256]{2,1,0:T(8,128)(2,1)S(1)}, u32[]{:S(2)}, u32[]{:S(2)}) collective-permute-start(bf16[8,64,256]{2,1,0:T(8,128)(2,1)} %copy-done.3), channel_id=1, source_target_pairs={{0,1},{1,0},{2,3},{3,2},{4,5},{5,4},{6,7},{7,6},{8,9},{9,8},{10,11... | collective-permute-start | bytes 786440 | tf_op jit(solution)/shard_map/ppermute | solution.py:114
  44.3 15.6 %collective-permute-start.14 = (bf16[8,64,256]{2,1,0:T(8,128)(2,1)S(1)}, bf16[8,64,256]{2,1,0:T(8,128)(2,1)S(1)}, u32[]{:S(2)}, u32[]{:S(2)}) collective-permute-start(bf16[8,64,256]{2,1,0:T(8,128)(2,1)S(1)} %collective-permute-done.13.refs_2_), channel_id=1, source_target_pairs={{0,1},{1,0},{2,3},{3,2},{4,5},{5,4},{6,7},{7,6},{8,9},{9,8},{10,11... | collective-permute-start | bytes 786440 | tf_op jit(solution)/shard_map/ppermute | solution.py:114
  44.8 11.2 %collective-permute-start.9 = (bf16[2,128,256]{2,1,0:T(8,128)(2,1)S(1)}, bf16[2,128,256]{2,1,0:T(8,128)(2,1)S(1)}, u32[]{:S(2)}, u32[]{:S(2)}) collective-permute-start(bf16[2,128,256]{2,1,0:T(8,128)(2,1)S(1)} %get-tuple-element.41.refs_4_), channel_id=1, source_target_pairs={{0,4},{4,0},{8,12},{12,8},{16,20},{20,16},{24,28},{28,24},{1,5},{5... | collective-permute-start | bytes 393224 | tf_op jit(solution)/shard_map/ppermute | solution.py:114
  49.6 6.4 %collective-permute-start.8 = (bf16[2,128,256]{2,1,0:T(8,128)(2,1)S(1)}, bf16[2,128,256]{2,1,0:T(8,128)(2,1)S(1)}, u32[]{:S(2)}, u32[]{:S(2)}) collective-permute-start(bf16[2,128,256]{2,1,0:T(8,128)(2,1)S(1)} %get-tuple-element.40.refs_2_), channel_id=1, source_target_pairs={{0,4},{4,0},{8,12},{12,8},{16,20},{20,16},{24,28},{28,24},{1,5},{5... | collective-permute-start | bytes 393224 | tf_op jit(solution)/shard_map/ppermute | solution.py:114
  50.9 7.0 %collective-permute-start.11 = (bf16[2,128,256]{2,1,0:T(8,128)(2,1)S(1)}, bf16[2,128,256]{2,1,0:T(8,128)(2,1)S(1)}, u32[]{:S(2)}, u32[]{:S(2)}) collective-permute-start(bf16[2,128,256]{2,1,0:T(8,128)(2,1)S(1)} %collective-permute-done.10.refs_6_), channel_id=1, source_target_pairs={{0,4},{4,0},{8,12},{12,8},{16,20},{20,16},{24,28},{28,24},{1,5},{5... | collective-permute-start | bytes 393224 | tf_op jit(solution)/shard_map/ppermute | solution.py:114
  59.9 1.0 %copy-start.4 = (bf16[8,64,256]{2,1,0:T(8,128)(2,1)S(1)}, bf16[8,64,256]{2,1,0:T(8,128)(2,1)}, u32[]{:S(2)}) copy-start(bf16[8,64,256]{2,1,0:T(8,128)(2,1)} %copy-done.3) | copy-start | bytes 786436
  60.9 0.7 copy-start.11
where the time goes:
time: 67.2 us; the launch traced here: 66.7 us
  starting transfers between devices  29.8 us (44%)
  waiting for transfers between devices  13.8 us (21%)
  Pallas kernels  13.4 us (20%)
  local copies, waits for them, and re-layouts  8.12 us (12%)
  between operations  0.83 us (1%)
  other arithmetic  0.78 us (1%)
    ppermute x13, starting transfers between devices, partners(): lax.ppermute(value, axis, [(source, source ^ bits) for source in range(co...  15.6 us
    ppermute x13, waiting for transfers between devices, partners(): lax.ppermute(value, axis, [(source, source ^ bits) for source in range(co...  10.2 us
    all_to_all x1, starting transfers between devices, gathered_form(): lax.all_to_all(jnp.broadcast_to(own, (R,) + own.shape[1:]), 'rows', 0, 0,...  7.25 us
    unnamed x28, local copies, waits for them, and re-layouts  5.99 us
    pallas_call x1, Pallas kernels, gathered_form(): call(functools.partial(slab_kernel, F, J, R, T, slot), [((R * T * slot, C...  5.28 us
    all_to_all x1, starting transfers between devices, gathered_form(): lax.all_to_all(later['packed'].reshape(R * T, slot, C), ('rows', 'tm'), 0...  4.42 us
    all_to_all x1, waiting for transfers between devices, gathered_form(): lax.all_to_all(jnp.broadcast_to(own, (R,) + own.shape[1:]), 'rows', 0, 0,...  3.65 us
    pallas_call x1, Pallas kernels, gathered_form(): call(functools.partial(weight_kernel, F, J, R, T, part), [((27, part, C),...  3.43 us
  transfers between devices with their start and end apart: 17, of which 5 were waited for; matrix products, arithmetic and copies ran while one was open for 2% of the time, Pallas kernels for 12%

commit v1 on v0

--- a/solution.py
+++ b/solution.py
@@ -121,7 +121,7 @@
         if k & (k - 1) == 0:
             blocks[k] = partners(value, axis, k)
     if gate is not None:
-        held = [k for k in blocks if k > 1]
+        held = [k for k in blocks if k > 0]
         blocks.update(zip(held, gate([blocks[k] for k in held])))
     for k in range(1, count):
         low = k & -k
@@ -347,7 +347,8 @@
 
 
 def finish_kernel(F, R, T, used, place, received, *refs):
-    latent, gain = refs[-2:]
+    latent, gain, token = refs[-3:]
+    token[...] = jnp.zeros_like(token)
     block = place[1]
     slot = received.shape[2]
     jl = used // F
@@ -517,10 +518,10 @@
     grad_all = exchanged(grad_rows, "tm")
 
     packed = lax.all_to_all(later["packed"].reshape(R * T, slot, C), ("rows", "tm"), 0, 0, tiled=True)
-    latent, gain_grad = call(
+    latent, gain_grad, token = call(
         functools.partial(finish_kernel, F, R, T, used),
-        [((span, C), bf16), ((1, part), f32)],
-        [], R * slot * C, R * slot * C, "sv" + "a" * (R // 2) + "vv",
+        [((span, C), bf16), ((1, part), f32), ((8, 128), f32)],
+        [], R * slot * C, R * slot * C, "sv" + "a" * (R // 2) + "vvv",
     )(place, packed.reshape(R, T, slot, C), *hidden_all[1::2])
 
     grads, bias_sum = call(
@@ -528,7 +529,7 @@
         [((2, R, (F * T + 2) * J, C), bf16), ((1, part), f32)],
         [],
         90 * WORK * span * C, 2 * R * T * span * C, "sa" + "v" * (T + 2),
-    )(place, gain_grad, *grad_all)
+    )(place, token, *grad_all)
     (weight_grad,) = call(
         functools.partial(weight_kernel, F, J, R, T, part),
         [((27, part, C), f32)],

time: 67.2 us -> 65.2 us (0.970)
  waiting for transfers between devices: 13.8 us -> 13.1 us
  starting transfers between devices: 29.8 us -> 29.1 us
    ppermute x13, waiting for transfers between devices: 10.2 us -> 9.12 us  [partners(): lax.ppermute(value, axis, [(source, source ^ bits) for source in range(co...]
    all_to_all x1, starting transfers between devices: 4.42 us -> 3.73 us  [gathered_form(): lax.all_to_all(later['packed'].reshape(R * T, slot, C), ('rows', 'tm'), 0...]
    unnamed x28 -> x26, local copies, waits for them, and re-layouts: 5.99 us -> 5.33 us
  transfers between devices with their start and end apart: 17 -> 17, of which waited for: 5 -> 5; matrix products, arithmetic and copies ran while one was open for 2% -> 2% of each run, Pallas kernels for 12% -> 13%
where the time goes in v1:
time: 65.2 us; the launch traced here: 64.7 us
  starting transfers between devices  29.1 us (45%)
  Pallas kernels  13.4 us (21%)
  waiting for transfers between devices  13.1 us (20%)
  local copies, waits for them, and re-layouts  7.46 us (11%)
  between operations  0.82 us (1%)
  other arithmetic  0.78 us (1%)
    ppermute x13, starting transfers between devices, partners(): lax.ppermute(value, axis, [(source, source ^ bits) for source in range(co...  15.5 us
    ppermute x13, waiting for transfers between devices, partners(): lax.ppermute(value, axis, [(source, source ^ bits) for source in range(co...  9.12 us
    all_to_all x1, starting transfers between devices, gathered_form(): lax.all_to_all(jnp.broadcast_to(own, (R,) + own.shape[1:]), 'rows', 0, 0,...  7.25 us
    unnamed x26, local copies, waits for them, and re-layouts  5.33 us
    pallas_call x1, Pallas kernels, gathered_form(): call(functools.partial(slab_kernel, F, J, R, T, slot), [((R * T * slot, C...  5.28 us
    all_to_all x1, starting transfers between devices, gathered_form(): lax.all_to_all(later['packed'].reshape(R * T, slot, C), ('rows', 'tm'), 0...  3.73 us
    all_to_all x1, waiting for transfers between devices, gathered_form(): lax.all_to_all(jnp.broadcast_to(own, (R,) + own.shape[1:]), 'rows', 0, 0,...  3.65 us
    pallas_call x1, Pallas kernels, gathered_form(): call(functools.partial(weight_kernel, F, J, R, T, part), [((27, part, C),...  3.43 us
  transfers between devices with their start and end apart: 17, of which 5 were waited for; matrix products, arithmetic and copies ran while one was open for 2% of the time, Pallas kernels for 13%

profile of v1, /device:TPU:0, one launch (start us, length us, event | category | flops | bytes accessed | tf_op | source)
XLA Modules:
  0.0 64.7 jit_solution(17507983456392865553)
XLA Ops:
  0.6 0.8 %broadcast_in_dim.7 = bf16[64,256]{1,0:T(8,128)(2,1)S(1)} reshape(bf16[4,8,2,256]{3,2,1,0:T(2,128)(2,1)} %param.9) | data formatting | bytes 65536 | tf_op jit(solution)/shard_map/broadcast_in_dim | solution.py:462
  1.4 0.7 %broadcast_in_dim.8 = bf16[8,64,256]{2,1,0:T(8,128)(2,1)} broadcast(bf16[64,256]{1,0:T(8,128)(2,1)S(1)} %broadcast_in_dim.7), dimensions={1,2} | broadcast | bytes 294912 | tf_op jit(solution)/shard_map/broadcast_in_dim | solution.py:462
  2.1 7.3 %all-to-all-start = ((bf16[8,64,256]{2,1,0:T(8,128)(2,1)}), bf16[8,64,256]{2,1,0:T(8,128)(2,1)S(1)}, u32[]{:S(2)}, u32[]{:S(2)}) async-start(bf16[8,64,256]{2,1,0:T(8,128)(2,1)} %broadcast_in_dim.8), calls=%async_computation | async-start | bytes 524288 | tf_op jit(solution)/shard_map/all_to_all | solution.py:461
  9.4 0.1 pad_add_fusion.place
  9.5 0.7 %pad_maximum_fusion.vectors = f32[2,256]{1,0:T(2,128)S(1)} fusion(f32[1,256]{1,0:T(1,128)} %bitcast.16, f32[1,256]{1,0:T(1,128)} %bitcast.17), kind=kLoop, calls=%fused_computation | loop fusion | flops 512 | bytes 4096 | tf_op jit(solution)/shard_map/stack | solution.py:455
  10.2 0.0 copy-start.10
  10.2 0.9 %copy-done.10 = bf16[4,2,32,256]{3,2,1,0:T(8,128)(2,1)S(1)} copy-done((bf16[4,2,32,256]{3,2,1,0:T(8,128)(2,1)S(1)}, bf16[4,2,32,256]{3,2,1,0:T(8,128)(2,1)}, u32[]{:S(2)}) %copy-start.10) | copy-done | bytes 131096
  11.1 0.8 %shard_map.92 = (bf16[2,2,64,256]{3,2,1,0:T(8,128)(2,1)S(1)}, bf16[256,256]{1,0:T(8,128)(2,1)S(1)}, f32[2,256]{1,0:T(2,128)S(1)}, bf16[128,128]{1,0:T(8,128)(2,1...) custom-call(s32[2]{0:T(128)S(1)} %pad_add_fusion.place, ...), custom_call_target="tpu_custom_call" | custom-call | flops 1179648000 | bytes 262144 | tf_op jit(solution)/shard_map/pallas_call | solution.py:466
  11.9 0.0 copy-start.7
  11.9 0.6 copy-done.7
  12.5 0.0 copy-start.2
  12.5 0.0 collective-permute-start
  12.5 1.6 %collective-permute-start.2 = (bf16[384,128]{1,0:T(8,128)(2,1)S(1)}, bf16[384,128]{1,0:T(8,128)(2,1)S(1)}, u32[]{:S(2)}, u32[]{:S(2)}) collective-permute-start(bf16[384,128]{1,0:T(8,128)(2,1)S(1)} %get-tuple-element.32), channel_id=1, source_target_pairs={{0,3},{1,2},{2,1},{3,0},{4,7},{5,6},{6,5},{7,4},{8,11},{9,10},{10,... | collective-permute-start | bytes 294920 | tf_op jit(solution)/shard_map/ppermute | solution.py:114
  14.1 0.5 collective-permute-start.1
  14.7 3.6 %all-to-all-done.grad_rows = bf16[8,64,256]{2,1,0:T(8,128)(2,1)S(1)} async-done(((bf16[8,64,256]{2,1,0:T(8,128)(2,1)}), bf16[8,64,256]{2,1,0:T(8,128)(2,1)S(1)}, u32[]{:S(2)}, u32[]{:S(2)}) %all-to-all-start) | async-done | bytes 262176 | tf_op jit(solution)/shard_map/all_to_all | solution.py:461
  18.3 0.0 copy-start.3
  18.3 1.3 %collective-permute-start.4 = (bf16[8,32,256]{2,1,0:T(8,128)(2,1)S(1)}, bf16[8,32,256]{2,1,0:T(8,128)(2,1)S(1)}, u32[]{:S(2)}, u32[]{:S(2)}) collective-permute-start(bf16[8,32,256]{2,1,0:T(8,128)(2,1)S(1)} %get-tuple-element.38), channel_id=1, source_target_pairs={{1,0},{2,1},{3,2},{5,4},{6,5},{7,6},{9,8},{10,9},{11,10},{13,12},{... | collective-permute-start | bytes 393224 | tf_op jit(solution)/shard_map/ppermute | solution.py:20
  19.6 0.0 collective-permute-done.1.refs_2_
  19.7 0.0 collective-permute-done.refs_1_
  19.7 0.0 collective-permute-done.2.refs_3_
  19.7 0.0 copy-done.8
  19.7 0.6 shard_map.93
  20.3 0.0 copy-start.6
  20.3 0.6 copy-done.6
  21.0 1.3 %collective-permute-start.3 = (bf16[2,96,256]{2,1,0:T(8,128)(2,1)S(1)}, bf16[2,96,256]{2,1,0:T(8,128)(2,1)S(1)}, u32[]{:S(2)}, u32[]{:S(2)}) collective-permute-start(bf16[2,96,256]{2,1,0:T(8,128)(2,1)S(1)} %get-tuple-element.34), channel_id=1, source_target_pairs={{4,0},{8,4},{12,8},{16,12},{20,16},{24,20},{28,24},{5,1},{9,5},{13... | collective-permute-start | bytes 294920 | tf_op jit(solution)/shard_map/ppermute | solution.py:20
  22.2 3.7 %collective-permute-start.7 = (bf16[2,128,256]{2,1,0:T(8,128)(2,1)S(1)}, bf16[2,128,256]{2,1,0:T(8,128)(2,1)S(1)}, u32[]{:S(2)}, u32[]{:S(2)}) collective-permute-start(bf16[2,128,256]{2,1,0:T(8,128)(2,1)S(1)} %get-tuple-element.40.refs_0_), channel_id=1, source_target_pairs={{0,16},{4,20},{8,24},{12,28},{16,0},{20,4},{24,8},{28,12},{1,17},{... | collective-permute-start | bytes 393224 | tf_op jit(solution)/shard_map/ppermute | solution.py:114
  26.0 1.5 %collective-permute-start.6 = (bf16[2,128,256]{2,1,0:T(8,128)(2,1)S(1)}, bf16[2,128,256]{2,1,0:T(8,128)(2,1)S(1)}, u32[]{:S(2)}, u32[]{:S(2)}) collective-permute-start(bf16[2,128,256]{2,1,0:T(8,128)(2,1)S(1)} %get-tuple-element.40.refs_0_), channel_id=1, source_target_pairs={{0,8},{4,12},{8,0},{12,4},{16,24},{20,28},{24,16},{28,20},{1,9},{5... | collective-permute-start | bytes 393224 | tf_op jit(solution)/shard_map/ppermute | solution.py:114
  27.4 0.6 collective-permute-start.5
  28.0 0.4 collective-permute-done.3.under
  28.4 1.8 %collective-permute-start.13 = (bf16[8,64,256]{2,1,0:T(8,128)(2,1)S(1)}, bf16[8,64,256]{2,1,0:T(8,128)(2,1)S(1)}, u32[]{:S(2)}, u32[]{:S(2)}) collective-permute-start(bf16[8,64,256]{2,1,0:T(8,128)(2,1)S(1)} %get-tuple-element.37.gathered.refs_0_), channel_id=1, source_target_pairs={{0,2},{1,3},{2,0},{3,1},{4,6},{5,7},{6,4},{7,5},{8,10},{9,11},{10,... | collective-permute-start | bytes 786440 | tf_op jit(solution)/shard_map/ppermute | solution.py:114
  30.2 0.0 collective-permute-done.4.following
  30.2 0.0 copy-done.2
  30.2 0.0 copy-done.5
  30.2 0.0 copy-done.3
  30.2 0.0 copy-done.12
  30.2 0.6 copy-done.11
  30.9 5.3 %shard_map.95 = (bf16[512,256]{1,0:T(8,128)(2,1)}, bf16[256,256]{1,0:T(8,128)(2,1)}) custom-call(s32[2]{0:T(128)} %copy-done.8, bf16[2,2,64,256]{3,2,1,0:T(8,128)(2,1)} %copy-done.5, bf16[2,2,32,256]{3,2,1,0:T(8,128)(2,1)} %copy-done.6, bf16[2,96,256]{2,1,0:T(8,128)(2,1)} %copy-done.12, bf16[27,256,256]{2,1,0:T(8,128)(2,1)} %bitcast.15, ...), custom_call_target="tpu_custom_call" | custom-call | flops 452984832 | bytes 3538944 | tf_op jit(solution)/shard_map/pallas_call | solution.py:491
  36.1 0.0 collective-permute-done.7.refs_3_
  36.2 0.0 collective-permute-done.6.refs_2_
  36.2 0.0 collective-permute-done.5.refs_1_
  36.2 0.0 copy-start
  36.2 0.9 %copy-done = bf16[512,256]{1,0:T(8,128)(2,1)S(1)} copy-done((bf16[512,256]{1,0:T(8,128)(2,1)S(1)}, bf16[512,256]{1,0:T(8,128)(2,1)}, u32[]{:S(2)}) %copy-start) | copy-done | bytes 262168
  37.1 0.7 %copy-done.1 = bf16[512,256]{1,0:T(8,128)(2,1)} copy-done((bf16[512,256]{1,0:T(8,128)(2,1)}, bf16[512,256]{1,0:T(8,128)(2,1)S(1)}, u32[]{:S(2)}) %copy-start.1) | copy-done | bytes 262168
  37.8 3.7 %all-to-all-start.1 = ((bf16[32,16,256]{2,1,0:T(8,128)(2,1)}), bf16[32,16,256]{2,1,0:T(8,128)(2,1)S(1)}, u32[]{:S(2)}, u32[]{:S(2)}) async-start(bf16[32,16,256]{2,1,0:T(8,128)(2,1)} %bitcast.12), calls=%async_computation.1 | async-start | bytes 524288 | tf_op jit(solution)/shard_map/all_to_all | solution.py:520
  41.6 1.8 %collective-permute-start.10 = (bf16[2,128,256]{2,1,0:T(8,128)(2,1)S(1)}, bf16[2,128,256]{2,1,0:T(8,128)(2,1)S(1)}, u32[]{:S(2)}, u32[]{:S(2)}) collective-permute-start(bf16[2,128,256]{2,1,0:T(8,128)(2,1)S(1)} %get-tuple-element.44.refs_4_), channel_id=1, source_target_pairs={{0,8},{4,12},{8,0},{12,4},{16,24},{20,28},{24,16},{28,20},{1,9},{5... | collective-permute-start | bytes 393224 | tf_op jit(solution)/shard_map/ppermute | solution.py:114
  43.4 0.0 collective-permute-start.12
  43.4 0.0 collective-permute-done.13.refs_2_
  43.4 0.5 collective-permute-start.14
  43.9 1.5 %collective-permute-start.9 = (bf16[2,128,256]{2,1,0:T(8,128)(2,1)S(1)}, bf16[2,128,256]{2,1,0:T(8,128)(2,1)S(1)}, u32[]{:S(2)}, u32[]{:S(2)}) collective-permute-start(bf16[2,128,256]{2,1,0:T(8,128)(2,1)S(1)} %get-tuple-element.44.refs_4_), channel_id=1, source_target_pairs={{0,4},{4,0},{8,12},{12,8},{16,20},{20,16},{24,28},{28,24},{1,5},{5... | collective-permute-start | bytes 393224 | tf_op jit(solution)/shard_map/ppermute | solution.py:114
  45.4 0.6 collective-permute-start.8
  45.9 5.5 %collective-permute-done.10.refs_6_ = bf16[2,128,256]{2,1,0:T(8,128)(2,1)S(1)} collective-permute-done((bf16[2,128,256]{2,1,0:T(8,128)(2,1)S(1)}, bf16[2,128,256]{2,1,0:T(8,128)(2,1)S(1)}, u32[]{:S(2)}, u32[]{:S(2)}) %collective-permute-start.10) | collective-permute-done | bytes 131104 | tf_op jit(solution)/shard_map/ppermute | solution.py:114
  51.5 1.5 %collective-permute-start.11 = (bf16[2,128,256]{2,1,0:T(8,128)(2,1)S(1)}, bf16[2,128,256]{2,1,0:T(8,128)(2,1)S(1)}, u32[]{:S(2)}, u32[]{:S(2)}) collective-permute-start(bf16[2,128,256]{2,1,0:T(8,128)(2,1)S(1)} %collective-permute-done.10.refs_6_), channel_id=1, source_target_pairs={{0,4},{4,0},{8,12},{12,8},{16,20},{20,16},{24,28},{28,24},{1,5},{5... | collective-permute-start | bytes 393224 | tf_op jit(solution)/shard_map/ppermute | solution.py:114
  52.9 0.8 %collective-permute-done.8.refs_1_.refs_3_ = bf16[2,128,256]{2,1,0:T(8,128)(2,1)S(1)} collective-permute-done((bf16[2,128,256]{2,1,0:T(8,128)(2,1)S(1)}, bf16[2,128,256]{2,1,0:T(8,128)(2,1)S(1)}, u32[]{:S(2)}, u32[]{:S(2)}) %collective-permute-start.8) | collective-permute-done | bytes 131104 | tf_op jit(solution)/shard_map/ppermute | solution.py:114
  53.7 0.0 collective-permute-done.9.refs_2_.refs_5_
  53.7 2.8 %collective-permute-done.11.refs_3_.refs_7_ = bf16[2,128,256]{2,1,0:T(8,128)(2,1)S(1)} collective-permute-done((bf16[2,128,256]{2,1,0:T(8,128)(2,1)S(1)}, bf16[2,128,256]{2,1,0:T(8,128)(2,1)S(1)}, u32[]{:S(2)}, u32[]{:S(2)}) %collective-permute-start.11) | collective-permute-done | bytes 131104 | tf_op jit(solution)/shard_map/ppermute | solution.py:114
  56.5 0.0 all-to-all-done.1
  56.5 0.0 copy-done.9
  56.5 1.4 %shard_map.97 = (bf16[64,256]{1,0:T(8,128)(2,1)S(1)}, f32[1,64]{1,0:T(1,128)}, f32[8,128]{1,0:T(8,128)S(1)}) custom-call(s32[2]{0:T(128)S(1)} %copy-done.9, bf16[8,4,16,256]{3,2,1,0:T(8,128)(2,1)S(1)} %bitcast.13, bf16[2,128,256]{2,1,0:T(8,128)(2,1)S(1)} %get-tuple-element.42.refs_0_.refs_1_, ...), custom_call_target="tpu_custom_call" | custom-call | flops 32768 | bytes 32768 | tf_op jit(solution)/shard_map/pallas_call | solution.py:521
  57.9 0.6 reshape.43
  58.5 0.0 collective-permute-done.12.refs_1_
  58.5 0.0 collective-permute-done.14.refs_3_
  58.5 0.9 %copy-done.4 = bf16[8,64,256]{2,1,0:T(8,128)(2,1)S(1)} copy-done((bf16[8,64,256]{2,1,0:T(8,128)(2,1)S(1)}, bf16[8,64,256]{2,1,0:T(8,128)(2,1)}, u32[]{:S(2)}) %copy-start.4) | copy-done | bytes 262168
  59.5 1.8 %shard_map.98 = (bf16[2,8,288,256]{3,2,1,0:T(8,128)(2,1)S(1)}, f32[1,64]{1,0:T(1,128)}) custom-call(s32[2]{0:T(128)S(1)} %copy-done.9, f32[8,128]{1,0:T(8,128)S(1)} %get-tuple-element.47._, bf16[8,64,256]{2,1,0:T(8,128)(2,1)S(1)} %copy-done.4, bf16[8,64,256]{2,1,0:T(8,128)(2,1)S(1)} %collective-permute-done.12.refs_1_, ...), custom_call_target="tpu_custom_call" | custom-call | flops 1769472000 | bytes 1048576 | tf_op jit(solution)/shard_map/pallas_call | solution.py:527
  61.2 3.4 %shard_map.99 = f32[27,64,256]{2,1,0:T(8,128)} custom-call(s32[2]{0:T(128)S(1)} %copy-done.9, bf16[2,8,288,256]{3,2,1,0:T(8,128)(2,1)S(1)} %get-tuple-element.48.grads, bf16[2,128,256]{2,1,0:T(8,128)(2,1)S(1)} %get-tuple-element.40.refs_0_, bf16[2,128,256]{2,1,0:T(8,128)(2,1)S(1)} %get-tuple-element.42.refs_0_.refs_1_, ...), custom_call_target="tpu_custom_call" | custom-call | flops 3932160000 | bytes 3538944 | tf_op jit(solution)/shard_map/pallas_call | solution.py:533
  (9 shorter events, 0.0 us)
Async XLA Ops:
  2.1 16.2 %all-to-all-start = ((bf16[8,64,256]{2,1,0:T(8,128)(2,1)}), bf16[8,64,256]{2,1,0:T(8,128)(2,1)S(1)}, u32[]{:S(2)}, u32[]{:S(2)}) async-start(bf16[8,64,256]{2,1,0:T(8,128)(2,1)} %broadcast_in_dim.8), calls=%async_computation | async-start | bytes 524288 | tf_op jit(solution)/shard_map/all_to_all | solution.py:461
  9.5 10.2 %copy-start.8 = (s32[2]{0:T(128)}, s32[2]{0:T(128)S(1)}, u32[]{:S(2)}) copy-start(s32[2]{0:T(128)S(1)} %pad_add_fusion.place) | copy-start | bytes 28
  10.2 0.9 %copy-start.10 = (bf16[4,2,32,256]{3,2,1,0:T(8,128)(2,1)S(1)}, bf16[4,2,32,256]{3,2,1,0:T(8,128)(2,1)}, u32[]{:S(2)}) copy-start(bf16[4,2,32,256]{3,2,1,0:T(8,128)(2,1)} %param.5) | copy-start | bytes 393220
  11.9 0.6 copy-start.7
  12.5 17.7 %copy-start.2 = (bf16[256,256]{1,0:T(8,128)(2,1)}, bf16[256,256]{1,0:T(8,128)(2,1)S(1)}, u32[]{:S(2)}) copy-start(bf16[256,256]{1,0:T(8,128)(2,1)S(1)} %get-tuple-element.35._.frames) | copy-start | bytes 393220
  12.5 17.7 %copy-start.5 = (bf16[2,2,64,256]{3,2,1,0:T(8,128)(2,1)}, bf16[2,2,64,256]{3,2,1,0:T(8,128)(2,1)S(1)}, u32[]{:S(2)}) copy-start(bf16[2,2,64,256]{3,2,1,0:T(8,128)(2,1)S(1)} %get-tuple-element.28.planes) | copy-start | bytes 393220
  12.5 7.1 %collective-permute-start = (bf16[384,128]{1,0:T(8,128)(2,1)S(1)}, bf16[384,128]{1,0:T(8,128)(2,1)S(1)}, u32[]{:S(2)}, u32[]{:S(2)}) collective-permute-start(bf16[384,128]{1,0:T(8,128)(2,1)S(1)} %get-tuple-element.30), channel_id=1, source_target_pairs={{0,1},{1,0},{2,3},{3,2},{4,5},{5,4},{6,7},{7,6},{8,9},{9,8},{10,11... | collective-permute-start | bytes 294920 | tf_op jit(solution)/shard_map/ppermute | solution.py:114
  12.5 7.2 %collective-permute-start.2 = (bf16[384,128]{1,0:T(8,128)(2,1)S(1)}, bf16[384,128]{1,0:T(8,128)(2,1)S(1)}, u32[]{:S(2)}, u32[]{:S(2)}) collective-permute-start(bf16[384,128]{1,0:T(8,128)(2,1)S(1)} %get-tuple-element.32), channel_id=1, source_target_pairs={{0,3},{1,2},{2,1},{3,0},{4,7},{5,6},{6,5},{7,4},{8,11},{9,10},{10,... | collective-permute-start | bytes 294920 | tf_op jit(solution)/shard_map/ppermute | solution.py:114
  14.1 5.5 %collective-permute-start.1 = (bf16[128,128]{1,0:T(8,128)(2,1)S(1)}, bf16[128,128]{1,0:T(8,128)(2,1)S(1)}, u32[]{:S(2)}, u32[]{:S(2)}) collective-permute-start(bf16[128,128]{1,0:T(8,128)(2,1)S(1)} %get-tuple-element.31), channel_id=1, source_target_pairs={{0,2},{1,3},{2,0},{3,1},{4,6},{5,7},{6,4},{7,5},{8,10},{9,11},{10,... | collective-permute-start | bytes 98312 | tf_op jit(solution)/shard_map/ppermute | solution.py:114
  18.3 11.9 %copy-start.3 = (bf16[8,64,256]{2,1,0:T(8,128)(2,1)}, bf16[8,64,256]{2,1,0:T(8,128)(2,1)S(1)}, u32[]{:S(2)}) copy-start(bf16[8,64,256]{2,1,0:T(8,128)(2,1)S(1)} %get-tuple-element.37.gathered.refs_0_) | copy-start | bytes 786436
  18.3 11.9 %collective-permute-start.4 = (bf16[8,32,256]{2,1,0:T(8,128)(2,1)S(1)}, bf16[8,32,256]{2,1,0:T(8,128)(2,1)S(1)}, u32[]{:S(2)}, u32[]{:S(2)}) collective-permute-start(bf16[8,32,256]{2,1,0:T(8,128)(2,1)S(1)} %get-tuple-element.38), channel_id=1, source_target_pairs={{1,0},{2,1},{3,2},{5,4},{6,5},{7,6},{9,8},{10,9},{11,10},{13,12},{... | collective-permute-start | bytes 393224 | tf_op jit(solution)/shard_map/ppermute | solution.py:20
  20.3 0.6 copy-start.6
  21.0 7.4 %collective-permute-start.3 = (bf16[2,96,256]{2,1,0:T(8,128)(2,1)S(1)}, bf16[2,96,256]{2,1,0:T(8,128)(2,1)S(1)}, u32[]{:S(2)}, u32[]{:S(2)}) collective-permute-start(bf16[2,96,256]{2,1,0:T(8,128)(2,1)S(1)} %get-tuple-element.34), channel_id=1, source_target_pairs={{4,0},{8,4},{12,8},{16,12},{20,16},{24,20},{28,24},{5,1},{9,5},{13... | collective-permute-start | bytes 294920 | tf_op jit(solution)/shard_map/ppermute | solution.py:20
  22.2 13.9 %collective-permute-start.7 = (bf16[2,128,256]{2,1,0:T(8,128)(2,1)S(1)}, bf16[2,128,256]{2,1,0:T(8,128)(2,1)S(1)}, u32[]{:S(2)}, u32[]{:S(2)}) collective-permute-start(bf16[2,128,256]{2,1,0:T(8,128)(2,1)S(1)} %get-tuple-element.40.refs_0_), channel_id=1, source_target_pairs={{0,16},{4,20},{8,24},{12,28},{16,0},{20,4},{24,8},{28,12},{1,17},{... | collective-permute-start | bytes 393224 | tf_op jit(solution)/shard_map/ppermute | solution.py:114
  26.0 10.2 %collective-permute-start.6 = (bf16[2,128,256]{2,1,0:T(8,128)(2,1)S(1)}, bf16[2,128,256]{2,1,0:T(8,128)(2,1)S(1)}, u32[]{:S(2)}, u32[]{:S(2)}) collective-permute-start(bf16[2,128,256]{2,1,0:T(8,128)(2,1)S(1)} %get-tuple-element.40.refs_0_), channel_id=1, source_target_pairs={{0,8},{4,12},{8,0},{12,4},{16,24},{20,28},{24,16},{28,20},{1,9},{5... | collective-permute-start | bytes 393224 | tf_op jit(solution)/shard_map/ppermute | solution.py:114
  27.4 8.7 %collective-permute-start.5 = (bf16[2,128,256]{2,1,0:T(8,128)(2,1)S(1)}, bf16[2,128,256]{2,1,0:T(8,128)(2,1)S(1)}, u32[]{:S(2)}, u32[]{:S(2)}) collective-permute-start(bf16[2,128,256]{2,1,0:T(8,128)(2,1)S(1)} %get-tuple-element.40.refs_0_), channel_id=1, source_target_pairs={{0,4},{4,0},{8,12},{12,8},{16,20},{20,16},{24,28},{28,24},{1,5},{5... | collective-permute-start | bytes 393224 | tf_op jit(solution)/shard_map/ppermute | solution.py:114
  28.4 1.9 %copy-start.12 = (bf16[2,96,256]{2,1,0:T(8,128)(2,1)}, bf16[2,96,256]{2,1,0:T(8,128)(2,1)S(1)}, u32[]{:S(2)}) copy-start(bf16[2,96,256]{2,1,0:T(8,128)(2,1)S(1)} %collective-permute-done.3.under) | copy-start | bytes 294916
  28.4 15.1 %collective-permute-start.13 = (bf16[8,64,256]{2,1,0:T(8,128)(2,1)S(1)}, bf16[8,64,256]{2,1,0:T(8,128)(2,1)S(1)}, u32[]{:S(2)}, u32[]{:S(2)}) collective-permute-start(bf16[8,64,256]{2,1,0:T(8,128)(2,1)S(1)} %get-tuple-element.37.gathered.refs_0_), channel_id=1, source_target_pairs={{0,2},{1,3},{2,0},{3,1},{4,6},{5,7},{6,4},{7,5},{8,10},{9,11},{10,... | collective-permute-start | bytes 786440 | tf_op jit(solution)/shard_map/ppermute | solution.py:114
  30.2 0.7 %copy-start.11 = (bf16[8,32,256]{2,1,0:T(8,128)(2,1)}, bf16[8,32,256]{2,1,0:T(8,128)(2,1)S(1)}, u32[]{:S(2)}) copy-start(bf16[8,32,256]{2,1,0:T(8,128)(2,1)S(1)} %collective-permute-done.4.following) | copy-start | bytes 393220
  30.9 25.7 %copy-start.9 = (s32[2]{0:T(128)S(1)}, s32[2]{0:T(128)}, u32[]{:S(2)}) copy-start(s32[2]{0:T(128)} %copy-done.8) | copy-start | bytes 28
  36.2 1.0 %copy-start = (bf16[512,256]{1,0:T(8,128)(2,1)S(1)}, bf16[512,256]{1,0:T(8,128)(2,1)}, u32[]{:S(2)}) copy-start(bf16[512,256]{1,0:T(8,128)(2,1)} %get-tuple-element.39.refs_0_) | copy-start | bytes 786436
  37.1 0.7 %copy-start.1 = (bf16[512,256]{1,0:T(8,128)(2,1)}, bf16[512,256]{1,0:T(8,128)(2,1)S(1)}, u32[]{:S(2)}) copy-start(bf16[512,256]{1,0:T(8,128)(2,1)S(1)} %get-tuple-element.41) | copy-start | bytes 786436
  37.8 18.7 %all-to-all-start.1 = ((bf16[32,16,256]{2,1,0:T(8,128)(2,1)}), bf16[32,16,256]{2,1,0:T(8,128)(2,1)S(1)}, u32[]{:S(2)}, u32[]{:S(2)}) async-start(bf16[32,16,256]{2,1,0:T(8,128)(2,1)} %bitcast.12), calls=%async_computation.1 | async-start | bytes 524288 | tf_op jit(solution)/shard_map/all_to_all | solution.py:520
  41.6 9.9 %collective-permute-start.10 = (bf16[2,128,256]{2,1,0:T(8,128)(2,1)S(1)}, bf16[2,128,256]{2,1,0:T(8,128)(2,1)S(1)}, u32[]{:S(2)}, u32[]{:S(2)}) collective-permute-start(bf16[2,128,256]{2,1,0:T(8,128)(2,1)S(1)} %get-tuple-element.44.refs_4_), channel_id=1, source_target_pairs={{0,8},{4,12},{8,0},{12,4},{16,24},{20,28},{24,16},{28,20},{1,9},{5... | collective-permute-start | bytes 393224 | tf_op jit(solution)/shard_map/ppermute | solution.py:114
  43.4 15.1 %collective-permute-start.12 = (bf16[8,64,256]{2,1,0:T(8,128)(2,1)}, bf16[8,64,256]{2,1,0:T(8,128)(2,1)S(1)}, u32[]{:S(2)}, u32[]{:S(2)}) collective-permute-start(bf16[8,64,256]{2,1,0:T(8,128)(2,1)} %copy-done.3), channel_id=1, source_target_pairs={{0,1},{1,0},{2,3},{3,2},{4,5},{5,4},{6,7},{7,6},{8,9},{9,8},{10,11... | collective-permute-start | bytes 786440 | tf_op jit(solution)/shard_map/ppermute | solution.py:114
  43.4 15.1 %collective-permute-start.14 = (bf16[8,64,256]{2,1,0:T(8,128)(2,1)S(1)}, bf16[8,64,256]{2,1,0:T(8,128)(2,1)S(1)}, u32[]{:S(2)}, u32[]{:S(2)}) collective-permute-start(bf16[8,64,256]{2,1,0:T(8,128)(2,1)S(1)} %collective-permute-done.13.refs_2_), channel_id=1, source_target_pairs={{0,1},{1,0},{2,3},{3,2},{4,5},{5,4},{6,7},{7,6},{8,9},{9,8},{10,11... | collective-permute-start | bytes 786440 | tf_op jit(solution)/shard_map/ppermute | solution.py:114
  43.9 9.8 %collective-permute-start.9 = (bf16[2,128,256]{2,1,0:T(8,128)(2,1)S(1)}, bf16[2,128,256]{2,1,0:T(8,128)(2,1)S(1)}, u32[]{:S(2)}, u32[]{:S(2)}) collective-permute-start(bf16[2,128,256]{2,1,0:T(8,128)(2,1)S(1)} %get-tuple-element.44.refs_4_), channel_id=1, source_target_pairs={{0,4},{4,0},{8,12},{12,8},{16,20},{20,16},{24,28},{28,24},{1,5},{5... | collective-permute-start | bytes 393224 | tf_op jit(solution)/shard_map/ppermute | solution.py:114
  45.4 8.3 %collective-permute-start.8 = (bf16[2,128,256]{2,1,0:T(8,128)(2,1)S(1)}, bf16[2,128,256]{2,1,0:T(8,128)(2,1)S(1)}, u32[]{:S(2)}, u32[]{:S(2)}) collective-permute-start(bf16[2,128,256]{2,1,0:T(8,128)(2,1)S(1)} %get-tuple-element.43.refs_2_), channel_id=1, source_target_pairs={{0,4},{4,0},{8,12},{12,8},{16,20},{20,16},{24,28},{28,24},{1,5},{5... | collective-permute-start | bytes 393224 | tf_op jit(solution)/shard_map/ppermute | solution.py:114
  51.5 5.1 %collective-permute-start.11 = (bf16[2,128,256]{2,1,0:T(8,128)(2,1)S(1)}, bf16[2,128,256]{2,1,0:T(8,128)(2,1)S(1)}, u32[]{:S(2)}, u32[]{:S(2)}) collective-permute-start(bf16[2,128,256]{2,1,0:T(8,128)(2,1)S(1)} %collective-permute-done.10.refs_6_), channel_id=1, source_target_pairs={{0,4},{4,0},{8,12},{12,8},{16,20},{20,16},{24,28},{28,24},{1,5},{5... | collective-permute-start | bytes 393224 | tf_op jit(solution)/shard_map/ppermute | solution.py:114
  58.5 1.0 %copy-start.4 = (bf16[8,64,256]{2,1,0:T(8,128)(2,1)S(1)}, bf16[8,64,256]{2,1,0:T(8,128)(2,1)}, u32[]{:S(2)}) copy-start(bf16[8,64,256]{2,1,0:T(8,128)(2,1)} %copy-done.3) | copy-start | bytes 786436

commit v2 on v1

--- a/solution.py
+++ b/solution.py
@@ -502,22 +502,22 @@
         limit=VMEM_LIMIT_WIDE,
     )(place, planes, cached, under, weight, frames_copy, vectors, grad_rows, following)
 
-    later = {}
+    def after(blocks, values):
+        shapes = [(v.shape, bf16) for v in values]
+        first, count = len(blocks), len(values)
+        aliases = {first + n: n for n in range(count)}
+        places = "a" * (first + 2 * count)
+        return list(call(gate_kernel, shapes, [], 0, 0, places, aliases)(*blocks, *values))
 
     def after_slab(blocks):
-        through = [packed] + blocks
-        shapes = [(b.shape, bf16) for b in through]
-        count = len(through)
-        aliases = {n: n for n in range(count)}
-        later["packed"], *blocks = call(
-            gate_kernel, shapes, [], 0, 0, "a" * (2 * count), aliases
-        )(*through)
-        return blocks
+        return after([packed], blocks)
 
     hidden_all = exchanged(joined, "rows", after_slab)
     grad_all = exchanged(grad_rows, "tm")
 
-    packed = lax.all_to_all(later["packed"].reshape(R * T, slot, C), ("rows", "tm"), 0, 0, tiled=True)
+    two_steps = [hidden_all[k] for k in range(R) if k.bit_count() == 2]
+    (packed,) = after(two_steps, [packed])
+    packed = lax.all_to_all(packed.reshape(R * T, slot, C), ("rows", "tm"), 0, 0, tiled=True)
     latent, gain_grad, token = call(
         functools.partial(finish_kernel, F, R, T, used),
         [((span, C), bf16), ((1, part), f32), ((8, 128), f32)],

time: 65.2 us -> 67.6 us (1.037)
  waiting for transfers between devices: 13.1 us -> 18.3 us
  starting transfers between devices: 29.1 us -> 26.7 us
    all_to_all x1, waiting for transfers between devices: 0.01 us -> 2.59 us  [gathered_form(): lax.all_to_all(packed.reshape(R * T, slot, C), ('rows', 'tm'), 0, 0, tile...]
    ppermute x13, waiting for transfers between devices: 9.12 us -> 11 us  [partners(): lax.ppermute(value, axis, [(source, source ^ bits) for source in range(co...]
    ppermute x13, starting transfers between devices: 15.5 us -> 14.3 us  [partners(): lax.ppermute(value, axis, [(source, source ^ bits) for source in range(co...]
    all_to_all x1, starting transfers between devices: 3.73 us -> 2.59 us  [gathered_form(): lax.all_to_all(packed.reshape(R * T, slot, C), ('rows', 'tm'), 0, 0, tile...]
    ppermute x2, waiting for transfers between devices: 0.37 us -> 1.06 us  [shifted(): lax.ppermute(value, axis, [(source, source + steps) for source in range(l...]
  transfers between devices with their start and end apart: 17 -> 17, of which waited for: 5 -> 8; matrix products, arithmetic and copies ran while one was open for 2% -> 2% of each run, Pallas kernels for 13% -> 12%
where the time goes in v2:
time: 67.6 us; the launch traced here: 67.2 us
  starting transfers between devices  26.7 us (39%)
  waiting for transfers between devices  18.3 us (27%)
  Pallas kernels  13.4 us (20%)
  local copies, waits for them, and re-layouts  7.27 us (11%)
  other arithmetic  0.78 us (1%)
  between operations  0.78 us (1%)
    ppermute x13, starting transfers between devices, partners(): lax.ppermute(value, axis, [(source, source ^ bits) for source in range(co...  14.3 us
    ppermute x13, waiting for transfers between devices, partners(): lax.ppermute(value, axis, [(source, source ^ bits) for source in range(co...  11 us
    all_to_all x1, starting transfers between devices, gathered_form(): lax.all_to_all(jnp.broadcast_to(own, (R,) + own.shape[1:]), 'rows', 0, 0,...  7.25 us
    pallas_call x1, Pallas kernels, gathered_form(): call(functools.partial(slab_kernel, F, J, R, T, slot), [((R * T * slot, C...  5.31 us
    unnamed x26, local copies, waits for them, and re-layouts  5.14 us
    all_to_all x1, waiting for transfers between devices, gathered_form(): lax.all_to_all(jnp.broadcast_to(own, (R,) + own.shape[1:]), 'rows', 0, 0,...  3.65 us
    pallas_call x1, Pallas kernels, gathered_form(): call(functools.partial(weight_kernel, F, J, R, T, part), [((27, part, C),...  3.43 us
    all_to_all x1, waiting for transfers between devices, gathered_form(): lax.all_to_all(packed.reshape(R * T, slot, C), ('rows', 'tm'), 0, 0, tile...  2.59 us
  transfers between devices with their start and end apart: 17, of which 8 were waited for; matrix products, arithmetic and copies ran while one was open for 2% of the time, Pallas kernels for 12%

profile of v2, /device:TPU:0, one launch (start us, length us, event | category | flops | bytes accessed | tf_op | source)
XLA Modules:
  0.0 67.2 jit_solution(16152300711234804775)
XLA Ops:
  0.6 0.8 %broadcast_in_dim.7 = bf16[64,256]{1,0:T(8,128)(2,1)S(1)} reshape(bf16[4,8,2,256]{3,2,1,0:T(2,128)(2,1)} %param.9) | data formatting | bytes 65536 | tf_op jit(solution)/shard_map/broadcast_in_dim | solution.py:462
  1.4 0.7 %broadcast_in_dim.8 = bf16[8,64,256]{2,1,0:T(8,128)(2,1)} broadcast(bf16[64,256]{1,0:T(8,128)(2,1)S(1)} %broadcast_in_dim.7), dimensions={1,2} | broadcast | bytes 294912 | tf_op jit(solution)/shard_map/broadcast_in_dim | solution.py:462
  2.1 7.3 %all-to-all-start = ((bf16[8,64,256]{2,1,0:T(8,128)(2,1)}), bf16[8,64,256]{2,1,0:T(8,128)(2,1)S(1)}, u32[]{:S(2)}, u32[]{:S(2)}) async-start(bf16[8,64,256]{2,1,0:T(8,128)(2,1)} %broadcast_in_dim.8), calls=%async_computation | async-start | bytes 524288 | tf_op jit(solution)/shard_map/all_to_all | solution.py:461
  9.4 0.1 pad_add_fusion.place
  9.5 0.0 copy-start.8
  9.5 0.7 %pad_maximum_fusion.vectors = f32[2,256]{1,0:T(2,128)S(1)} fusion(f32[1,256]{1,0:T(1,128)} %bitcast.16, f32[1,256]{1,0:T(1,128)} %bitcast.17), kind=kLoop, calls=%fused_computation | loop fusion | flops 512 | bytes 4096 | tf_op jit(solution)/shard_map/stack | solution.py:455
  10.2 0.0 copy-start.10
  10.2 0.9 %copy-done.10 = bf16[4,2,32,256]{3,2,1,0:T(8,128)(2,1)S(1)} copy-done((bf16[4,2,32,256]{3,2,1,0:T(8,128)(2,1)S(1)}, bf16[4,2,32,256]{3,2,1,0:T(8,128)(2,1)}, u32[]{:S(2)}) %copy-start.10) | copy-done | bytes 131096
  11.1 0.8 %shard_map.92 = (bf16[2,2,64,256]{3,2,1,0:T(8,128)(2,1)S(1)}, bf16[256,256]{1,0:T(8,128)(2,1)S(1)}, f32[2,256]{1,0:T(2,128)S(1)}, bf16[128,128]{1,0:T(8,128)(2,1...) custom-call(s32[2]{0:T(128)S(1)} %pad_add_fusion.place, ...), custom_call_target="tpu_custom_call" | custom-call | flops 1179648000 | bytes 262144 | tf_op jit(solution)/shard_map/pallas_call | solution.py:466
  11.9 0.0 copy-start.7
  11.9 0.6 copy-done.7
  12.5 0.0 copy-start.2
  12.5 0.0 collective-permute-start
  12.5 1.6 %collective-permute-start.2 = (bf16[384,128]{1,0:T(8,128)(2,1)S(1)}, bf16[384,128]{1,0:T(8,128)(2,1)S(1)}, u32[]{:S(2)}, u32[]{:S(2)}) collective-permute-start(bf16[384,128]{1,0:T(8,128)(2,1)S(1)} %get-tuple-element.31), channel_id=1, source_target_pairs={{0,3},{1,2},{2,1},{3,0},{4,7},{5,6},{6,5},{7,4},{8,11},{9,10},{10,... | collective-permute-start | bytes 294920 | tf_op jit(solution)/shard_map/ppermute | solution.py:114
  14.1 0.5 collective-permute-start.1
  14.7 3.6 %all-to-all-done.grad_rows = bf16[8,64,256]{2,1,0:T(8,128)(2,1)S(1)} async-done(((bf16[8,64,256]{2,1,0:T(8,128)(2,1)}), bf16[8,64,256]{2,1,0:T(8,128)(2,1)S(1)}, u32[]{:S(2)}, u32[]{:S(2)}) %all-to-all-start) | async-done | bytes 262176 | tf_op jit(solution)/shard_map/all_to_all | solution.py:461
  18.3 0.0 copy-start.3
  18.3 0.7 %copy-done.3 = bf16[8,64,256]{2,1,0:T(8,128)(2,1)} copy-done((bf16[8,64,256]{2,1,0:T(8,128)(2,1)}, bf16[8,64,256]{2,1,0:T(8,128)(2,1)S(1)}, u32[]{:S(2)}) %copy-start.3) | copy-done | bytes 262168
  19.0 1.3 %collective-permute-start.4 = (bf16[8,32,256]{2,1,0:T(8,128)(2,1)S(1)}, bf16[8,32,256]{2,1,0:T(8,128)(2,1)S(1)}, u32[]{:S(2)}, u32[]{:S(2)}) collective-permute-start(bf16[8,32,256]{2,1,0:T(8,128)(2,1)S(1)} %get-tuple-element.37), channel_id=1, source_target_pairs={{1,0},{2,1},{3,2},{5,4},{6,5},{7,6},{9,8},{10,9},{11,10},{13,12},{... | collective-permute-start | bytes 393224 | tf_op jit(solution)/shard_map/ppermute | solution.py:20
  20.3 0.0 collective-permute-done.1.refs_2_
  20.3 0.0 collective-permute-done.refs_1_
  20.3 0.0 collective-permute-done.2.refs_3_
  20.4 0.0 copy-done.8
  20.4 0.6 shard_map.93
  21.0 0.0 copy-start.6
  21.0 0.6 copy-done.6
  21.6 1.3 %collective-permute-start.3 = (bf16[2,96,256]{2,1,0:T(8,128)(2,1)S(1)}, bf16[2,96,256]{2,1,0:T(8,128)(2,1)S(1)}, u32[]{:S(2)}, u32[]{:S(2)}) collective-permute-start(bf16[2,96,256]{2,1,0:T(8,128)(2,1)S(1)} %get-tuple-element.33), channel_id=1, source_target_pairs={{4,0},{8,4},{12,8},{16,12},{20,16},{24,20},{28,24},{5,1},{9,5},{13... | collective-permute-start | bytes 294920 | tf_op jit(solution)/shard_map/ppermute | solution.py:20
  22.9 3.1 %collective-permute-start.7 = (bf16[2,128,256]{2,1,0:T(8,128)(2,1)S(1)}, bf16[2,128,256]{2,1,0:T(8,128)(2,1)S(1)}, u32[]{:S(2)}, u32[]{:S(2)}) collective-permute-start(bf16[2,128,256]{2,1,0:T(8,128)(2,1)S(1)} %get-tuple-element.39.refs_0_), channel_id=1, source_target_pairs={{0,16},{4,20},{8,24},{12,28},{16,0},{20,4},{24,8},{28,12},{1,17},{... | collective-permute-start | bytes 393224 | tf_op jit(solution)/shard_map/ppermute | solution.py:114
  26.0 1.4 %collective-permute-start.6 = (bf16[2,128,256]{2,1,0:T(8,128)(2,1)S(1)}, bf16[2,128,256]{2,1,0:T(8,128)(2,1)S(1)}, u32[]{:S(2)}, u32[]{:S(2)}) collective-permute-start(bf16[2,128,256]{2,1,0:T(8,128)(2,1)S(1)} %get-tuple-element.39.refs_0_), channel_id=1, source_target_pairs={{0,8},{4,12},{8,0},{12,4},{16,24},{20,28},{24,16},{28,20},{1,9},{5... | collective-permute-start | bytes 393224 | tf_op jit(solution)/shard_map/ppermute | solution.py:114
  27.4 0.6 collective-permute-start.5
  28.0 1.1 %collective-permute-done.3.under = bf16[2,96,256]{2,1,0:T(8,128)(2,1)S(1)} collective-permute-done((bf16[2,96,256]{2,1,0:T(8,128)(2,1)S(1)}, bf16[2,96,256]{2,1,0:T(8,128)(2,1)S(1)}, u32[]{:S(2)}, u32[]{:S(2)}) %collective-permute-start.3) | collective-permute-done | bytes 98336 | tf_op jit(solution)/shard_map/ppermute | solution.py:20
  29.0 0.0 collective-permute-done.4.following
  29.0 0.0 copy-done.2
  29.0 0.0 copy-done.5
  29.1 0.6 copy-done.12
  29.7 0.1 copy-done.11
  29.7 5.3 %shard_map.95 = (bf16[512,256]{1,0:T(8,128)(2,1)}, bf16[256,256]{1,0:T(8,128)(2,1)}) custom-call(s32[2]{0:T(128)} %copy-done.8, bf16[2,2,64,256]{3,2,1,0:T(8,128)(2,1)} %copy-done.5, bf16[2,2,32,256]{3,2,1,0:T(8,128)(2,1)} %copy-done.6, bf16[2,96,256]{2,1,0:T(8,128)(2,1)} %copy-done.12, bf16[27,256,256]{2,1,0:T(8,128)(2,1)} %bitcast.15, ...), custom_call_target="tpu_custom_call" | custom-call | flops 452984832 | bytes 3538944 | tf_op jit(solution)/shard_map/pallas_call | solution.py:491
  35.1 0.1 collective-permute-done.7.refs_3_
  35.1 0.4 collective-permute-done.6.refs_2_
  35.5 0.0 collective-permute-done.5.refs_1_
  35.5 0.9 %copy-done = bf16[512,256]{1,0:T(8,128)(2,1)S(1)} copy-done((bf16[512,256]{1,0:T(8,128)(2,1)S(1)}, bf16[512,256]{1,0:T(8,128)(2,1)}, u32[]{:S(2)}) %copy-start) | copy-done | bytes 262168
  36.5 2.8 %collective-permute-start.8 = (bf16[2,128,256]{2,1,0:T(8,128)(2,1)S(1)}, bf16[2,128,256]{2,1,0:T(8,128)(2,1)S(1)}, u32[]{:S(2)}, u32[]{:S(2)}) collective-permute-start(bf16[2,128,256]{2,1,0:T(8,128)(2,1)S(1)} %get-tuple-element.40.refs_2_), channel_id=1, source_target_pairs={{0,4},{4,0},{8,12},{12,8},{16,20},{20,16},{24,28},{28,24},{1,5},{5... | collective-permute-start | bytes 393224 | tf_op jit(solution)/shard_map/ppermute | solution.py:114
  39.3 0.0 collective-permute-start.10
  39.3 0.0 collective-permute-start.9
  39.3 0.0 copy-done.4
  39.3 2.0 %collective-permute-start.13 = (bf16[8,64,256]{2,1,0:T(8,128)(2,1)S(1)}, bf16[8,64,256]{2,1,0:T(8,128)(2,1)S(1)}, u32[]{:S(2)}, u32[]{:S(2)}) collective-permute-start(bf16[8,64,256]{2,1,0:T(8,128)(2,1)S(1)} %copy-done.4), channel_id=1, source_target_pairs={{0,2},{1,3},{2,0},{3,1},{4,6},{5,7},{6,4},{7,5},{8,10},{9,11},{10,... | collective-permute-start | bytes 786440 | tf_op jit(solution)/shard_map/ppermute | solution.py:114
  41.3 2.2 %collective-permute-done.8.refs_0_.refs_1_.refs_3_ = bf16[2,128,256]{2,1,0:T(8,128)(2,1)S(1)} collective-permute-done((bf16[2,128,256]{2,1,0:T(8,128)(2,1)S(1)}, bf16[2,128,256]{2,1,0:T(8,128)(2,1)S(1)}, u32[]{:S(2)}, u32[]{:S(2)}) %collective-permute-start.8) | collective-permute-done | bytes 131104 | tf_op jit(solution)/shard_map/ppermute | solution.py:114
  43.5 1.2 %collective-permute-done.10.refs_2_.refs_6_ = bf16[2,128,256]{2,1,0:T(8,128)(2,1)S(1)} collective-permute-done((bf16[2,128,256]{2,1,0:T(8,128)(2,1)S(1)}, bf16[2,128,256]{2,1,0:T(8,128)(2,1)S(1)}, u32[]{:S(2)}, u32[]{:S(2)}) %collective-permute-start.10) | collective-permute-done | bytes 131104 | tf_op jit(solution)/shard_map/ppermute | solution.py:114
  44.7 1.3 %collective-permute-done.9.refs_1_.refs_2_.refs_5_ = bf16[2,128,256]{2,1,0:T(8,128)(2,1)S(1)} collective-permute-done((bf16[2,128,256]{2,1,0:T(8,128)(2,1)S(1)}, bf16[2,128,256]{2,1,0:T(8,128)(2,1)S(1)}, u32[]{:S(2)}, u32[]{:S(2)}) %collective-permute-start.9) | collective-permute-done | bytes 131104 | tf_op jit(solution)/shard_map/ppermute | solution.py:114
  46.1 0.7 %copy-done.1 = bf16[512,256]{1,0:T(8,128)(2,1)} copy-done((bf16[512,256]{1,0:T(8,128)(2,1)}, bf16[512,256]{1,0:T(8,128)(2,1)S(1)}, u32[]{:S(2)}) %copy-start.1) | copy-done | bytes 262168
  46.8 2.6 %all-to-all-start.1 = ((bf16[32,16,256]{2,1,0:T(8,128)(2,1)}), bf16[32,16,256]{2,1,0:T(8,128)(2,1)S(1)}, u32[]{:S(2)}, u32[]{:S(2)}) async-start(bf16[32,16,256]{2,1,0:T(8,128)(2,1)} %bitcast.12), calls=%async_computation.1 | async-start | bytes 524288 | tf_op jit(solution)/shard_map/all_to_all | solution.py:520
  49.4 0.2 collective-permute-start.12
  49.5 0.0 collective-permute-done.13.refs_2_
  49.5 0.4 collective-permute-start.14
  49.9 1.6 %collective-permute-start.11 = (bf16[2,128,256]{2,1,0:T(8,128)(2,1)S(1)}, bf16[2,128,256]{2,1,0:T(8,128)(2,1)S(1)}, u32[]{:S(2)}, u32[]{:S(2)}) collective-permute-start(bf16[2,128,256]{2,1,0:T(8,128)(2,1)S(1)} %collective-permute-done.10.refs_2_.refs_6_), channel_id=1, source_target_pairs={{0,4},{4,0},{8,12},{12,8},{16,20},{20,16},{24,28},{28,24},{1,5},{5... | collective-permute-start | bytes 393224 | tf_op jit(solution)/shard_map/ppermute | solution.py:114
  51.6 5.8 %collective-permute-done.11.refs_3_.refs_7_ = bf16[2,128,256]{2,1,0:T(8,128)(2,1)S(1)} collective-permute-done((bf16[2,128,256]{2,1,0:T(8,128)(2,1)S(1)}, bf16[2,128,256]{2,1,0:T(8,128)(2,1)S(1)}, u32[]{:S(2)}, u32[]{:S(2)}) %collective-permute-start.11) | collective-permute-done | bytes 131104 | tf_op jit(solution)/shard_map/ppermute | solution.py:114
  57.4 2.6 %all-to-all-done.1 = bf16[32,16,256]{2,1,0:T(8,128)(2,1)S(1)} async-done(((bf16[32,16,256]{2,1,0:T(8,128)(2,1)}), bf16[32,16,256]{2,1,0:T(8,128)(2,1)S(1)}, u32[]{:S(2)}, u32[]{:S(2)}) %all-to-all-start.1) | async-done | bytes 262176 | tf_op jit(solution)/shard_map/all_to_all | solution.py:520
  60.0 0.0 copy-done.9
  60.0 1.4 %shard_map.98 = (bf16[64,256]{1,0:T(8,128)(2,1)S(1)}, f32[1,64]{1,0:T(1,128)}, f32[8,128]{1,0:T(8,128)S(1)}) custom-call(s32[2]{0:T(128)S(1)} %copy-done.9, bf16[8,4,16,256]{3,2,1,0:T(8,128)(2,1)S(1)} %bitcast.13, bf16[2,128,256]{2,1,0:T(8,128)(2,1)S(1)} %get-tuple-element.42.refs_0_.refs_1_, ...), custom_call_target="tpu_custom_call" | custom-call | flops 32768 | bytes 32768 | tf_op jit(solution)/shard_map/pallas_call | solution.py:521
  61.3 0.6 reshape.43
  62.0 0.0 collective-permute-done.12.refs_1_
  62.0 0.0 collective-permute-done.14.refs_3_
  62.0 1.8 %shard_map.99 = (bf16[2,8,288,256]{3,2,1,0:T(8,128)(2,1)S(1)}, f32[1,64]{1,0:T(1,128)}) custom-call(s32[2]{0:T(128)S(1)} %copy-done.9, f32[8,128]{1,0:T(8,128)S(1)} %get-tuple-element.45._, bf16[8,64,256]{2,1,0:T(8,128)(2,1)S(1)} %copy-done.4, bf16[8,64,256]{2,1,0:T(8,128)(2,1)S(1)} %collective-permute-done.12.refs_1_, ...), custom_call_target="tpu_custom_call" | custom-call | flops 1769472000 | bytes 1048576 | tf_op jit(solution)/shard_map/pallas_call | solution.py:527
  63.7 3.4 %shard_map.100 = f32[27,64,256]{2,1,0:T(8,128)} custom-call(s32[2]{0:T(128)S(1)} %copy-done.9, bf16[2,8,288,256]{3,2,1,0:T(8,128)(2,1)S(1)} %get-tuple-element.46.grads, bf16[2,128,256]{2,1,0:T(8,128)(2,1)S(1)} %get-tuple-element.39.refs_0_, bf16[2,128,256]{2,1,0:T(8,128)(2,1)S(1)} %get-tuple-element.42.refs_0_.refs_1_, ...), custom_call_target="tpu_custom_call" | custom-call | flops 3932160000 | bytes 3538944 | tf_op jit(solution)/shard_map/pallas_call | solution.py:533
  (10 shorter events, 0.0 us)
Async XLA Ops:
  2.1 16.2 %all-to-all-start = ((bf16[8,64,256]{2,1,0:T(8,128)(2,1)}), bf16[8,64,256]{2,1,0:T(8,128)(2,1)S(1)}, u32[]{:S(2)}, u32[]{:S(2)}) async-start(bf16[8,64,256]{2,1,0:T(8,128)(2,1)} %broadcast_in_dim.8), calls=%async_computation | async-start | bytes 524288 | tf_op jit(solution)/shard_map/all_to_all | solution.py:461
  9.5 10.9 %copy-start.8 = (s32[2]{0:T(128)}, s32[2]{0:T(128)S(1)}, u32[]{:S(2)}) copy-start(s32[2]{0:T(128)S(1)} %pad_add_fusion.place) | copy-start | bytes 28
  10.2 0.9 %copy-start.10 = (bf16[4,2,32,256]{3,2,1,0:T(8,128)(2,1)S(1)}, bf16[4,2,32,256]{3,2,1,0:T(8,128)(2,1)}, u32[]{:S(2)}) copy-start(bf16[4,2,32,256]{3,2,1,0:T(8,128)(2,1)} %param.5) | copy-start | bytes 393220
  11.9 0.6 copy-start.7
  12.5 16.5 %copy-start.2 = (bf16[256,256]{1,0:T(8,128)(2,1)}, bf16[256,256]{1,0:T(8,128)(2,1)S(1)}, u32[]{:S(2)}) copy-start(bf16[256,256]{1,0:T(8,128)(2,1)S(1)} %get-tuple-element.34._.frames) | copy-start | bytes 393220
  12.5 16.5 %copy-start.5 = (bf16[2,2,64,256]{3,2,1,0:T(8,128)(2,1)}, bf16[2,2,64,256]{3,2,1,0:T(8,128)(2,1)S(1)}, u32[]{:S(2)}) copy-start(bf16[2,2,64,256]{3,2,1,0:T(8,128)(2,1)S(1)} %get-tuple-element.27.planes) | copy-start | bytes 393220
  12.5 7.8 %collective-permute-start = (bf16[384,128]{1,0:T(8,128)(2,1)S(1)}, bf16[384,128]{1,0:T(8,128)(2,1)S(1)}, u32[]{:S(2)}, u32[]{:S(2)}) collective-permute-start(bf16[384,128]{1,0:T(8,128)(2,1)S(1)} %get-tuple-element.29), channel_id=1, source_target_pairs={{0,1},{1,0},{2,3},{3,2},{4,5},{5,4},{6,7},{7,6},{8,9},{9,8},{10,11... | collective-permute-start | bytes 294920 | tf_op jit(solution)/shard_map/ppermute | solution.py:114
  12.5 7.8 %collective-permute-start.2 = (bf16[384,128]{1,0:T(8,128)(2,1)S(1)}, bf16[384,128]{1,0:T(8,128)(2,1)S(1)}, u32[]{:S(2)}, u32[]{:S(2)}) collective-permute-start(bf16[384,128]{1,0:T(8,128)(2,1)S(1)} %get-tuple-element.31), channel_id=1, source_target_pairs={{0,3},{1,2},{2,1},{3,0},{4,7},{5,6},{6,5},{7,4},{8,11},{9,10},{10,... | collective-permute-start | bytes 294920 | tf_op jit(solution)/shard_map/ppermute | solution.py:114
  14.1 6.2 %collective-permute-start.1 = (bf16[128,128]{1,0:T(8,128)(2,1)S(1)}, bf16[128,128]{1,0:T(8,128)(2,1)S(1)}, u32[]{:S(2)}, u32[]{:S(2)}) collective-permute-start(bf16[128,128]{1,0:T(8,128)(2,1)S(1)} %get-tuple-element.30), channel_id=1, source_target_pairs={{0,2},{1,3},{2,0},{3,1},{4,6},{5,7},{6,4},{7,5},{8,10},{9,11},{10,... | collective-permute-start | bytes 98312 | tf_op jit(solution)/shard_map/ppermute | solution.py:114
  18.3 0.7 %copy-start.3 = (bf16[8,64,256]{2,1,0:T(8,128)(2,1)}, bf16[8,64,256]{2,1,0:T(8,128)(2,1)S(1)}, u32[]{:S(2)}) copy-start(bf16[8,64,256]{2,1,0:T(8,128)(2,1)S(1)} %get-tuple-element.36.gathered.refs_0_) | copy-start | bytes 786436
  19.0 10.0 %collective-permute-start.4 = (bf16[8,32,256]{2,1,0:T(8,128)(2,1)S(1)}, bf16[8,32,256]{2,1,0:T(8,128)(2,1)S(1)}, u32[]{:S(2)}, u32[]{:S(2)}) collective-permute-start(bf16[8,32,256]{2,1,0:T(8,128)(2,1)S(1)} %get-tuple-element.37), channel_id=1, source_target_pairs={{1,0},{2,1},{3,2},{5,4},{6,5},{7,6},{9,8},{10,9},{11,10},{13,12},{... | collective-permute-start | bytes 393224 | tf_op jit(solution)/shard_map/ppermute | solution.py:20
  21.0 0.6 copy-start.6
  21.6 7.4 %collective-permute-start.3 = (bf16[2,96,256]{2,1,0:T(8,128)(2,1)S(1)}, bf16[2,96,256]{2,1,0:T(8,128)(2,1)S(1)}, u32[]{:S(2)}, u32[]{:S(2)}) collective-permute-start(bf16[2,96,256]{2,1,0:T(8,128)(2,1)S(1)} %get-tuple-element.33), channel_id=1, source_target_pairs={{4,0},{8,4},{12,8},{16,12},{20,16},{24,20},{28,24},{5,1},{9,5},{13... | collective-permute-start | bytes 294920 | tf_op jit(solution)/shard_map/ppermute | solution.py:20
  22.9 12.2 %collective-permute-start.7 = (bf16[2,128,256]{2,1,0:T(8,128)(2,1)S(1)}, bf16[2,128,256]{2,1,0:T(8,128)(2,1)S(1)}, u32[]{:S(2)}, u32[]{:S(2)}) collective-permute-start(bf16[2,128,256]{2,1,0:T(8,128)(2,1)S(1)} %get-tuple-element.39.refs_0_), channel_id=1, source_target_pairs={{0,16},{4,20},{8,24},{12,28},{16,0},{20,4},{24,8},{28,12},{1,17},{... | collective-permute-start | bytes 393224 | tf_op jit(solution)/shard_map/ppermute | solution.py:114
  26.0 9.5 %collective-permute-start.6 = (bf16[2,128,256]{2,1,0:T(8,128)(2,1)S(1)}, bf16[2,128,256]{2,1,0:T(8,128)(2,1)S(1)}, u32[]{:S(2)}, u32[]{:S(2)}) collective-permute-start(bf16[2,128,256]{2,1,0:T(8,128)(2,1)S(1)} %get-tuple-element.39.refs_0_), channel_id=1, source_target_pairs={{0,8},{4,12},{8,0},{12,4},{16,24},{20,28},{24,16},{28,20},{1,9},{5... | collective-permute-start | bytes 393224 | tf_op jit(solution)/shard_map/ppermute | solution.py:114
  27.4 8.1 %collective-permute-start.5 = (bf16[2,128,256]{2,1,0:T(8,128)(2,1)S(1)}, bf16[2,128,256]{2,1,0:T(8,128)(2,1)S(1)}, u32[]{:S(2)}, u32[]{:S(2)}) collective-permute-start(bf16[2,128,256]{2,1,0:T(8,128)(2,1)S(1)} %get-tuple-element.39.refs_0_), channel_id=1, source_target_pairs={{0,4},{4,0},{8,12},{12,8},{16,20},{20,16},{24,28},{28,24},{1,5},{5... | collective-permute-start | bytes 393224 | tf_op jit(solution)/shard_map/ppermute | solution.py:114
  29.0 0.6 copy-start.12
  29.0 0.7 %copy-start.11 = (bf16[8,32,256]{2,1,0:T(8,128)(2,1)}, bf16[8,32,256]{2,1,0:T(8,128)(2,1)S(1)}, u32[]{:S(2)}) copy-start(bf16[8,32,256]{2,1,0:T(8,128)(2,1)S(1)} %collective-permute-done.4.following) | copy-start | bytes 393220
  29.7 9.6 %copy-start.4 = (bf16[8,64,256]{2,1,0:T(8,128)(2,1)S(1)}, bf16[8,64,256]{2,1,0:T(8,128)(2,1)}, u32[]{:S(2)}) copy-start(bf16[8,64,256]{2,1,0:T(8,128)(2,1)} %copy-done.3) | copy-start | bytes 786436
  29.7 30.2 %copy-start.9 = (s32[2]{0:T(128)S(1)}, s32[2]{0:T(128)}, u32[]{:S(2)}) copy-start(s32[2]{0:T(128)} %copy-done.8) | copy-start | bytes 28
  35.5 1.0 %copy-start = (bf16[512,256]{1,0:T(8,128)(2,1)S(1)}, bf16[512,256]{1,0:T(8,128)(2,1)}, u32[]{:S(2)}) copy-start(bf16[512,256]{1,0:T(8,128)(2,1)} %get-tuple-element.38.refs_0_.refs_3_) | copy-start | bytes 786436
  36.5 7.1 %collective-permute-start.8 = (bf16[2,128,256]{2,1,0:T(8,128)(2,1)S(1)}, bf16[2,128,256]{2,1,0:T(8,128)(2,1)S(1)}, u32[]{:S(2)}, u32[]{:S(2)}) collective-permute-start(bf16[2,128,256]{2,1,0:T(8,128)(2,1)S(1)} %get-tuple-element.40.refs_2_), channel_id=1, source_target_pairs={{0,4},{4,0},{8,12},{12,8},{16,20},{20,16},{24,28},{28,24},{1,5},{5... | collective-permute-start | bytes 393224 | tf_op jit(solution)/shard_map/ppermute | solution.py:114
  39.3 5.4 %collective-permute-start.10 = (bf16[2,128,256]{2,1,0:T(8,128)(2,1)S(1)}, bf16[2,128,256]{2,1,0:T(8,128)(2,1)S(1)}, u32[]{:S(2)}, u32[]{:S(2)}) collective-permute-start(bf16[2,128,256]{2,1,0:T(8,128)(2,1)S(1)} %get-tuple-element.41.refs_4_), channel_id=1, source_target_pairs={{0,8},{4,12},{8,0},{12,4},{16,24},{20,28},{24,16},{28,20},{1,9},{5... | collective-permute-start | bytes 393224 | tf_op jit(solution)/shard_map/ppermute | solution.py:114
  39.3 6.8 %collective-permute-start.9 = (bf16[2,128,256]{2,1,0:T(8,128)(2,1)S(1)}, bf16[2,128,256]{2,1,0:T(8,128)(2,1)S(1)}, u32[]{:S(2)}, u32[]{:S(2)}) collective-permute-start(bf16[2,128,256]{2,1,0:T(8,128)(2,1)S(1)} %get-tuple-element.41.refs_4_), channel_id=1, source_target_pairs={{0,4},{4,0},{8,12},{12,8},{16,20},{20,16},{24,28},{28,24},{1,5},{5... | collective-permute-start | bytes 393224 | tf_op jit(solution)/shard_map/ppermute | solution.py:114
  39.3 10.2 %collective-permute-start.13 = (bf16[8,64,256]{2,1,0:T(8,128)(2,1)S(1)}, bf16[8,64,256]{2,1,0:T(8,128)(2,1)S(1)}, u32[]{:S(2)}, u32[]{:S(2)}) collective-permute-start(bf16[8,64,256]{2,1,0:T(8,128)(2,1)S(1)} %copy-done.4), channel_id=1, source_target_pairs={{0,2},{1,3},{2,0},{3,1},{4,6},{5,7},{6,4},{7,5},{8,10},{9,11},{10,... | collective-permute-start | bytes 786440 | tf_op jit(solution)/shard_map/ppermute | solution.py:114
  46.1 0.7 %copy-start.1 = (bf16[512,256]{1,0:T(8,128)(2,1)}, bf16[512,256]{1,0:T(8,128)(2,1)S(1)}, u32[]{:S(2)}) copy-start(bf16[512,256]{1,0:T(8,128)(2,1)S(1)} %shard_map.97) | copy-start | bytes 786436
  46.8 13.2 %all-to-all-start.1 = ((bf16[32,16,256]{2,1,0:T(8,128)(2,1)}), bf16[32,16,256]{2,1,0:T(8,128)(2,1)S(1)}, u32[]{:S(2)}, u32[]{:S(2)}) async-start(bf16[32,16,256]{2,1,0:T(8,128)(2,1)} %bitcast.12), calls=%async_computation.1 | async-start | bytes 524288 | tf_op jit(solution)/shard_map/all_to_all | solution.py:520
  49.4 12.6 %collective-permute-start.12 = (bf16[8,64,256]{2,1,0:T(8,128)(2,1)S(1)}, bf16[8,64,256]{2,1,0:T(8,128)(2,1)S(1)}, u32[]{:S(2)}, u32[]{:S(2)}) collective-permute-start(bf16[8,64,256]{2,1,0:T(8,128)(2,1)S(1)} %copy-done.4), channel_id=1, source_target_pairs={{0,1},{1,0},{2,3},{3,2},{4,5},{5,4},{6,7},{7,6},{8,9},{9,8},{10,11... | collective-permute-start | bytes 786440 | tf_op jit(solution)/shard_map/ppermute | solution.py:114
  49.5 12.4 %collective-permute-start.14 = (bf16[8,64,256]{2,1,0:T(8,128)(2,1)S(1)}, bf16[8,64,256]{2,1,0:T(8,128)(2,1)S(1)}, u32[]{:S(2)}, u32[]{:S(2)}) collective-permute-start(bf16[8,64,256]{2,1,0:T(8,128)(2,1)S(1)} %collective-permute-done.13.refs_2_), channel_id=1, source_target_pairs={{0,1},{1,0},{2,3},{3,2},{4,5},{5,4},{6,7},{7,6},{8,9},{9,8},{10,11... | collective-permute-start | bytes 786440 | tf_op jit(solution)/shard_map/ppermute | solution.py:114
  49.9 7.4 %collective-permute-start.11 = (bf16[2,128,256]{2,1,0:T(8,128)(2,1)S(1)}, bf16[2,128,256]{2,1,0:T(8,128)(2,1)S(1)}, u32[]{:S(2)}, u32[]{:S(2)}) collective-permute-start(bf16[2,128,256]{2,1,0:T(8,128)(2,1)S(1)} %collective-permute-done.10.refs_2_.refs_6_), channel_id=1, source_target_pairs={{0,4},{4,0},{8,12},{12,8},{16,20},{20,16},{24,28},{28,24},{1,5},{5... | collective-permute-start | bytes 393224 | tf_op jit(solution)/shard_map/ppermute | solution.py:114
